TPU v7x, 32 devices: a whole 2x2x4 slice. The times are simulated.
32 devices in a mesh: dp: 2 (over x), expert: 16 (over z, y, core).
Axes of the slice: x: 2, y: 2, z: 4, core: 2. Of those that a mesh axis runs over, the one named last changes fastest.
Arguments:
- tokens: bfloat16 [256, 4096], P(('dp', 'expert')), may hold values from -6 to 6
- cotangent: bfloat16 [256, 4096], P(('dp', 'expert')), may hold values from -6 to 6
- gates: float32 [256, 8], P(('dp', 'expert')), may hold values from 0.1 to 0.5
- expert_ids: int32 [256, 8], P(('dp', 'expert')), may hold values from 0 to 15, all different within a row; in each aligned block of 8 rows (0 to 7, 8 to 15, ...) at most 8 rows name the same one
- swap_flag: int32 [16], replicated, may hold values from 0 to 1, as said below
- w_in: bfloat16 [16, 2, 768, 4096], P('expert', None, 'dp'), may hold values from -0.09375 to 0.09375
- w_down: bfloat16 [16, 768, 4096], P('expert', 'dp'), may hold values from -0.21875 to 0.21875
Outputs:
- mixed: bfloat16 [256, 4096], P(('dp', 'expert'))
- grad_tokens: bfloat16 [256, 4096], P(('dp', 'expert'))
- grad_in: bfloat16 [16, 2, 768, 4096], P('expert', None, 'dp')
- grad_down: bfloat16 [16, 768, 4096], P('expert', 'dp')
Inputs may be any that keep to these rules, and one draw needn't show every extreme that they name: `expert_ids`: each row names 8 different experts; in the rows of one device no expert is named more than 8 times. swap_flag[e] equals swap_flag[(e + 8) mod 16]; both values occur.
All inputs are finite; a program needn't handle non-finite values.
Results may differ from a plain program's by a relative error of at most 0.014.
Values may be sent and summed in bfloat16 or wider, within the bound.
No kernel may reach another device: no remote copies, remote signals or barrier semaphores. Data moves between devices by JAX's collectives and lax.ppermute only.
A program may use at most 128 MiB of HBM per device.

v0:
```python
import functools

import jax
import jax.numpy as jnp
from jax import lax
from jax.experimental import pallas as pl
from jax.experimental.pallas import tpu as pltpu
from jax.sharding import PartitionSpec as P

F32, BF16 = jnp.float32, jnp.bfloat16
ANY = pl.BlockSpec(memory_space=pl.ANY)
SMEM = pl.BlockSpec(memory_space=pltpu.SMEM)
VMEM = pl.BlockSpec(memory_space=pltpu.VMEM)
CHUNKS = 4
ROW_BLOCK = 256
STAGE_MIB = 40


def nt(a, b):
    return lax.dot_general(a, b, (((1,), (1,)), ((), ())), preferred_element_type=F32)


def nn(a, b):
    return jnp.dot(a, b, preferred_element_type=F32)


def each_rows(total, body):
    if total <= ROW_BLOCK:
        body(pl.ds(0, total))
    else:

        @pl.loop(0, total // ROW_BLOCK)
        def _(i):
            body(pl.ds(pl.multiple_of(i * ROW_BLOCK, ROW_BLOCK), ROW_BLOCK))


def columns(dim):
    step = dim // CHUNKS
    return [pl.ds(c * step, step) for c in range(CHUNKS)]


def started(sems, base, pairs):
    copies = [
        pltpu.make_async_copy(source, target, sems.at[base + i])
        for i, (source, target) in enumerate(pairs)
    ]
    for copy in copies:
        copy.start()
    return copies


def wait(copies):
    for copy in copies:
        copy.wait()


def row_copies(own, received, buffer, cols, target=None):
    half = own.shape[0]
    target = cols if target is None else target
    return [
        (own.at[:, cols], buffer.at[pl.ds(0, half), target]),
        (received.at[:, cols], buffer.at[pl.ds(half, half), target]),
    ]


def split_three(x):
    high = x.astype(BF16)
    rest = x - high.astype(F32)
    middle = rest.astype(BF16)
    low = (rest - middle.astype(F32)).astype(BF16)
    return high, middle, low


def gate_column(parts, expert, experts):
    lane = lax.broadcasted_iota(jnp.int32, parts.shape, 1)
    values = parts.astype(F32)
    high, middle, low = (
        jnp.sum(jnp.where(lane == expert + i * experts, values, 0.0), axis=1, keepdims=True)
        for i in range(3)
    )
    return (low + middle) + high


def fill_gates(parts, gate, expert, experts):
    def body(rows):
        column = gate_column(parts[rows, :], expert, experts)
        gate[rows, :] = jnp.broadcast_to(column, (column.shape[0], gate.shape[1]))

    each_rows(parts.shape[0], body)


def held_expert(flags):
    me = lax.axis_index("expert")
    flag = flags[me]
    return me, jnp.where(flag > 0, me ^ (lax.axis_size("expert") // 2), me), flag


def zero_kernel(*refs):
    refs[-1][...] = jnp.zeros_like(refs[-1])


def stage_kernel(after, weight, out, sems):
    wait(started(sems, 0, [(weight.at[:, c], out.at[:, c]) for c in columns(weight.shape[1])]))


def hidden_kernel(xa, xb, win, after, act, silu, slope, zero, x, hidden, sems):
    units, rows_all = act.shape
    dim = win.shape[1]
    loads = []
    for c, cols in enumerate(columns(dim)):
        loads.append(started(sems, 2 * c, row_copies(xa, xb, x, cols)))
    zero[...] = jnp.zeros_like(zero)
    for c, cols in enumerate(columns(dim)):
        wait(loads[c])

        def multiply(rows):
            product = nt(win[:, cols], x[rows, cols])
            hidden[:, rows] = product if c == 0 else hidden[:, rows] + product

        each_rows(rows_all, multiply)

    def pointwise(rows):
        g, u = hidden[pl.ds(0, units), rows], hidden[pl.ds(units, units), rows]
        sig = jax.nn.sigmoid(g)
        gated = g * sig
        silu[:, rows] = gated
        slope[:, rows] = u * sig * (1.0 + g * (1.0 - sig))
        act[:, rows] = (gated * u).astype(BF16)

    each_rows(rows_all, pointwise)


def split_product(rows_ref, weight, keep0, keep1, send, finish):
    half, dim = send.shape
    for c, cols in enumerate(columns(dim)):
        keep = (keep0, keep1)[c * 2 // CHUNKS]
        inner = pl.ds(cols.start % (dim // 2), cols.size)

        def multiply(start, target, place):
            def body(rows):
                mine = pl.ds(rows.start + start, rows.size)
                target[rows, place] = finish(mine, nn(rows_ref[mine, :], weight[:, cols]).astype(BF16))

            return body

        each_rows(half, multiply(half, send, cols))
        each_rows(half, multiply(0, keep, inner))


def part_kernel(
    experts, flags, xa, xb, act, wdown, after, keep0, keep1, send, gate, gate_held,
    parts, rows_act, sems,
):
    dim, width = wdown.shape[1], parts.shape[1]
    rows_all = parts.shape[0]
    loads = started(sems, 0, row_copies(xa, xb, parts, pl.ds(dim, width), pl.ds(0, width)))

    def turn(rows):
        rows_act[rows, :] = act[:, rows].T

    each_rows(rows_all, turn)
    me, held, _ = held_expert(flags)
    wait(loads)
    fill_gates(parts, gate, me, experts)
    fill_gates(parts, gate_held, held, experts)

    def weighted(rows, part):
        return (gate[rows, pl.ds(0, 1)] * part.astype(F32)).astype(BF16)

    split_product(rows_act, wdown, keep0, keep1, send, weighted)


def factor_kernel(ya, yb, silu, slope, gate, wdown, after, grad, y, total, sems):
    units, dim = wdown.shape
    rows_all = y.shape[0]
    loads = []
    for c, cols in enumerate(columns(dim)):
        loads.append(started(sems, 2 * c, row_copies(ya, yb, y, cols)))
    for c, cols in enumerate(columns(dim)):
        wait(loads[c])

        def multiply(rows):
            scaled = (gate[rows, pl.ds(0, 1)] * y[rows, cols].astype(F32)).astype(BF16)
            product = nt(wdown[:, cols], scaled)
            total[:, rows] = product if c == 0 else total[:, rows] + product

        each_rows(rows_all, multiply)

    def pointwise(rows):
        value = total[:, rows]
        for i, factor in enumerate((slope, silu)):
            grad[pl.ds(i * units, units), rows] = (value * factor[:, rows]).astype(BF16)

    each_rows(rows_all, pointwise)


def back_kernel(grad, win, keep0, keep1, send, rows_grad):
    def turn(rows):
        rows_grad[rows, :] = grad[:, rows].T

    each_rows(rows_grad.shape[0], turn)
    split_product(rows_grad, win, keep0, keep1, send, lambda rows, part: part)


def weight_kernel(
    scaled, flags, own, away, gate, ra, rb, *rest
):
    grads, r, used, out, sems = rest[-5:]
    groups, units, dim = grads.shape
    rows_all = r.shape[0]
    base, loads, stores = 0, [], []
    for cols in columns(dim):
        loads.append(started(sems, base, row_copies(ra, rb, r, cols)))
        base += 2
    _, _, flag = held_expert(flags)
    used[...] = jnp.where(flag > 0, away[...], own[...])
    for c, cols in enumerate(columns(dim)):
        wait(loads[c])
        if scaled:

            def scale(rows):
                r[rows, cols] = (gate[rows, pl.ds(0, 1)] * r[rows, cols].astype(F32)).astype(BF16)

            each_rows(rows_all, scale)
        pairs = []
        for i in range(groups):
            some = pl.ds(i * units, units)
            out[some, cols] = nn(used[some, :], r[:, cols]).astype(BF16)
            pairs.append((out.at[some, cols], grads.at[i, :, cols]))
        stores.append(started(sems, base, pairs))
        base += groups
    for store in stores:
        wait(store)


def rounded_up(value, unit):
    return -(-value // unit) * unit


def params(mib):
    return pltpu.CompilerParams(vmem_limit_bytes=mib * 1024 * 1024)


def cost(flops, size):
    return pl.CostEstimate(flops=flops, bytes_accessed=size, transcendentals=0)


def masks(axis):
    size, out = lax.axis_size(axis), []
    while size > 1:
        size //= 2
        out.append((axis, size))
    return out


def partner(block, bit):
    axis, mask = bit
    return lax.ppermute(block, axis, [(i, i ^ mask) for i in range(lax.axis_size(axis))])


def inner_rows(bit, done, order, unit):
    for other in done:
        if order.index(other) > order.index(bit):
            unit *= 2
    return unit


def join(a, b, inner):
    pair = [part.reshape(-1, inner, part.shape[-1]) for part in (a, b)]
    return jnp.concatenate(pair, axis=1).reshape(-1, a.shape[-1])


def halves(block, inner):
    split = block.reshape(-1, 2, inner, block.shape[1])
    return [split[:, i].reshape(-1, block.shape[1]) for i in (0, 1)]


def is_set(bit):
    return (lax.axis_index(bit[0]) & bit[1]) > 0


def add(a, b):
    return (a.astype(F32) + b.astype(F32)).astype(BF16)


def on_device(tokens, cotangent, gates, expert_ids, swap_flag, w_in, w_down):
    experts = lax.axis_size("expert")
    half_axis = experts // 2
    tok_dev, dim = tokens.shape
    units = w_down.shape[1]

    across, within = masks("dp"), masks("expert")
    core, near, far = within[-1], within[-2:-1], within[:-2]
    first = near + across
    second = across + near
    order = first[::-1] + far[::-1]
    rows_all = tok_dev * lax.axis_size("dp") * experts
    top = far[0]

    slots = jnp.arange(experts, dtype=jnp.int32)
    dense = jnp.sum(
        jnp.where(expert_ids[:, :, None] == slots, gates[:, :, None], 0.0), axis=1
    )
    parts = jnp.concatenate(split_three(dense), axis=1)
    width = rounded_up(parts.shape[1], 128)
    parts = jnp.pad(parts, ((0, 0), (0, width - parts.shape[1])))
    payload = jnp.concatenate([tokens, parts], axis=1)

    def far_gather(block, seen):
        for i in range(0, len(far), 2):
            group = far[i : i + 2]
            a = group[0]
            if len(group) == 2:
                b = group[1]
                fours = [
                    block,
                    partner(block, b),
                    partner(block, a),
                    partner(block, ("expert", a[1] | b[1])),
                ]
                seen.append(fours[1])
                pairs = [jnp.concatenate(fours[:2]), jnp.concatenate(fours[2:])]
            else:
                pairs = [block, partner(block, a)]
                seen.append(pairs[1])
            if a == top:
                turn = is_set(top)
                pairs = [jnp.where(turn, pairs[1 - j], pairs[j]) for j in (0, 1)]
            block = jnp.concatenate(pairs)
        return block

    def zero_after(*arrays):
        return pl.pallas_call(
            zero_kernel,
            out_shape=jax.ShapeDtypeStruct((16, dim // 2), BF16),
            in_specs=[ANY] * len(arrays),
            out_specs=VMEM,
            compiler_params=params(2),
            name="zero",
        )(*arrays)[:1]

    def plane_steps(block, zero=None):
        sides = [block[:, : dim // 2], block[:, dim // 2 :]]
        steps = []
        for k in range(len(first)):
            for i, route in enumerate((first, second)):
                bit = route[k]
                inner = inner_rows(bit, route[:k], order, far_rows)
                got = partner(sides[i], bit)
                if zero is not None and k == len(first) - 1:
                    got = got + zero()
                sides[i] = join(sides[i], got, inner)
            steps.append(list(sides))
        return steps

    def stage(after, weight, name):
        return pl.pallas_call(
            stage_kernel,
            out_shape=jax.ShapeDtypeStruct(weight.shape, BF16),
            in_specs=[ANY] * 2,
            out_specs=VMEM,
            scratch_shapes=[pltpu.SemaphoreType.DMA((CHUNKS,))],
            compiler_params=params(STAGE_MIB),
            cost_estimate=cost(0, 4 * weight.size),
            name=name,
        )(after, weight)

    seen = []
    x_far = far_gather(payload, seen)
    win = stage(seen[0], w_in.reshape(2 * units, dim), "stage_in")
    wdown = stage(seen[0], w_down.reshape(units, dim), "stage_down")
    far_rows = x_far.shape[0]
    x_steps = plane_steps(x_far)
    row = zero_after(x_steps[0][0])
    y_far = far_gather(cotangent + jnp.concatenate([row, row], axis=1), seen)
    xa = jnp.concatenate(x_steps[-1], axis=1)
    xb = partner(xa, core)

    half_rows = rows_all // 2
    limit = 60 if rows_all > 512 else 24
    rows_out = [
        jax.ShapeDtypeStruct((half_rows, dim // 2), BF16),
        jax.ShapeDtypeStruct((half_rows, dim // 2), BF16),
        jax.ShapeDtypeStruct((half_rows, dim), BF16),
    ]
    gate_type = jax.ShapeDtypeStruct((rows_all, 128), F32)
    saved_type = jax.ShapeDtypeStruct((units, rows_all), F32)
    product = 2 * rows_all * units * dim
    act, silu, slope, zero = pl.pallas_call(
        hidden_kernel,
        out_shape=[
            jax.ShapeDtypeStruct((units, rows_all), BF16),
            saved_type,
            saved_type,
            jax.ShapeDtypeStruct((16, dim // 2), BF16),
        ],
        in_specs=[ANY, ANY, VMEM, ANY],
        out_specs=[VMEM] * 4,
        scratch_shapes=[
            pltpu.VMEM((rows_all, dim), BF16),
            pltpu.VMEM((2 * units, rows_all), F32),
            pltpu.SemaphoreType.DMA((2 * CHUNKS,)),
        ],
        compiler_params=params(limit),
        cost_estimate=cost(2 * product, 4 * dim * (units + rows_all)),
        name="hidden",
    )(xa, xb, win, wdown)
    far_act = partner(act, ("expert", half_axis))
    ya = jnp.concatenate(plane_steps(y_far, lambda: zero[:1])[-1], axis=1)
    yb = partner(ya, core)
    *mixed_rows, gate, gate_held = pl.pallas_call(
        functools.partial(part_kernel, experts),
        out_shape=[*rows_out, gate_type, gate_type],
        in_specs=[SMEM, ANY, ANY, VMEM, VMEM, ANY],
        out_specs=[VMEM] * 5,
        scratch_shapes=[
            pltpu.VMEM((rows_all, width), BF16),
            pltpu.VMEM((rows_all, units), BF16),
            pltpu.SemaphoreType.DMA((2,)),
        ],
        compiler_params=params(limit),
        cost_estimate=cost(product, 2 * dim * (units + rows_all)),
        name="part",
    )(swap_flag, xa, xb, act, wdown, ya)
    grad = pl.pallas_call(
        factor_kernel,
        out_shape=jax.ShapeDtypeStruct((2 * units, rows_all), BF16),
        in_specs=[ANY] * 2 + [VMEM] * 4 + [ANY],
        out_specs=VMEM,
        scratch_shapes=[
            pltpu.VMEM((rows_all, dim), BF16),
            pltpu.VMEM((units, rows_all), F32),
            pltpu.SemaphoreType.DMA((2 * CHUNKS,)),
        ],
        compiler_params=params(limit),
        cost_estimate=cost(product, 2 * dim * (units + rows_all)),
        name="factors",
    )(ya, yb, silu, slope, gate, wdown, mixed_rows[2])
    far_grad = partner(grad, ("expert", half_axis))
    back_rows = pl.pallas_call(
        back_kernel,
        out_shape=rows_out,
        in_specs=[VMEM] * 2,
        out_specs=[VMEM] * 3,
        scratch_shapes=[pltpu.VMEM((rows_all, 2 * units), BF16)],
        compiler_params=params(limit),
        cost_estimate=cost(2 * product, 4 * dim * (units + rows_all)),
        name="back",
    )(grad, win)

    def added(keep, got, bit, left):
        inner = inner_rows(bit, left, order, tok_dev)
        return [add(*pair) for pair in zip(halves(keep, inner), halves(got, inner))]

    def far_sends(keep, groups):
        group = groups[-1]
        a = group[0]
        inner = keep.shape[0] // 2
        pair = [keep[:inner], keep[inner:]]
        if a == top:
            turn = is_set(top)
            pair = [jnp.where(turn, pair[1 - j], pair[j]) for j in (0, 1)]
        if len(group) == 1:
            return pair[0], [(pair[1], a[1])]
        b = group[1]
        low = inner // 2
        return pair[0][:low], [
            (pair[0][low:], b[1]),
            (pair[1][:low], a[1]),
            (pair[1][low:], a[1] | b[1]),
        ]

    def far_sum(mine, sends):
        arrived = [partner(rows, ("expert", mask)) for rows, mask in sends]
        total = mine.astype(F32)
        for rows in arrived:
            total = total + rows.astype(F32)
        return total.astype(BF16), arrived[0]

    groups = [far[i : i + 2] for i in range(0, len(far), 2)]
    routes = first[::-1], second[::-1]

    def core_sum(parts):
        got = partner(parts[2], core)
        return [parts[0], parts[1]], [got[:, : dim // 2], got[:, dim // 2 :]]

    keeps, gots = zip(core_sum(mixed_rows), core_sum(back_rows))
    sent = [None, None]
    zero = None
    for k in range(len(first)):
        for n in (0, 1):
            sent[n] = []
            for i, route in enumerate(routes):
                got = gots[n][i] if zero is None or n else gots[n][i] + zero
                left = set(order) - set(route[: k + 1])
                keeps[n][i], out = added(keeps[n][i], got, route[k], left)
                sent[n].append(out)
            for i, route in enumerate(routes):
                gots[n][i] = partner(sent[n][i], route[k])
        zero = zero_after(*sent[1])

    def plane_end(n, zero):
        return jnp.concatenate(
            [add(keep, got + zero) for keep, got in zip(keeps[n], gots[n])], axis=1
        )

    mine, sends = far_sends(plane_end(0, zero), groups)
    zero = zero_after(*[rows for rows, _ in sends])
    mixed, _ = far_sum(mine, sends)
    mine, sends = far_sends(plane_end(1, zero), groups)
    behind = [rows for rows, _ in sends]
    grad_tokens, back_near = far_sum(mine, sends)
    for group in groups[-2::-1]:
        mixed, _ = far_sum(*far_sends(mixed, [group]))
        grad_tokens, back_near = far_sum(*far_sends(grad_tokens, [group]))

    def weight_gradient(after, own, away, pieces, scaled, name):
        groups = own.shape[0] // units
        return pl.pallas_call(
            functools.partial(weight_kernel, scaled),
            out_shape=jax.ShapeDtypeStruct((groups, units, dim), BF16),
            in_specs=[SMEM] + [VMEM] * 3 + [ANY] * (2 + len(after)),
            out_specs=ANY,
            scratch_shapes=[
                pltpu.VMEM((rows_all, dim), BF16),
                pltpu.VMEM(own.shape, BF16),
                pltpu.VMEM((groups * units, dim), BF16),
                pltpu.SemaphoreType.DMA(((2 + groups) * CHUNKS,)),
            ],
            compiler_params=params(limit),
            cost_estimate=cost(
                2 * rows_all * groups * units * dim, 2 * dim * (groups * units + rows_all)
            ),
            name=name,
        )(swap_flag, own, away, gate_held, *pieces, *after)

    new_down = weight_gradient(behind, act, far_act, (ya, yb), True, "grad_down")
    new_in = weight_gradient([back_near], grad, far_grad, (xa, xb), False, "grad_in")
    return (mixed, grad_tokens, new_in.reshape(w_in.shape), new_down.reshape(w_down.shape))


def solution(mesh):
    rows = P(("dp", "expert"), None)
    w_in, w_down = P("expert", None, "dp", None), P("expert", "dp", None)
    return jax.shard_map(
        on_device,
        mesh=mesh,
        in_specs=(rows, rows, rows, rows, P(), w_in, w_down),
        out_specs=(rows, rows, w_in, w_down),
        check_vma=False,
    )
```

profile of v0, /device:TPU:0, one launch (start us, length us, event | category | flops | bytes accessed | tf_op | source)
XLA Modules:
  0.0 103.8 jit_solution(11702734820202677658)
XLA Ops:
  2.4 4.0 %collective-permute-start = (bf16[8,4224]{1,0:T(8,128)(2,1)S(1)}, bf16[8,4224]{1,0:T(8,128)(2,1)S(1)}, u32[]{:S(2)}, u32[]{:S(2)}) collective-permute-start(bf16[8,4224]{1,0:T(8,128)(2,1)S(1)} %pad_maximum_fusion.13), channel_id=1, source_target_pairs={{0,8},{1,9},{2,10},{3,11},{4,12},{5,13},{6,14},{7,15},{8,0},{9,1},... | collective-permute-start | bytes 202760 | tf_op jit(solution)/shard_map/ppermute | solution.py:258
  9.6 4.6 %collective-permute-done.1 = bf16[8,4224]{1,0:T(8,128)(2,1)S(1)} collective-permute-done((bf16[8,4224]{1,0:T(8,128)(2,1)S(1)}, bf16[8,4224]{1,0:T(8,128)(2,1)S(1)}, u32[]{:S(2)}, u32[]{:S(2)}) %collective-permute-start.1) | collective-permute-done | bytes 67616 | tf_op jit(solution)/shard_map/ppermute | solution.py:258
  15.2 1.6 %collective-permute-start.3 = (bf16[32,2048]{1,0:T(8,128)(2,1)S(1)}, bf16[32,2048]{1,0:T(8,128)(2,1)S(1)}, u32[]{:S(2)}, u32[]{:S(2)}) collective-permute-start(bf16[32,2048]{1,0:T(8,128)(2,1)S(1)} %pad_maximum_fusion.11), channel_id=1, source_target_pairs={{0,2},{1,3},{2,0},{3,1},{4,6},{5,7},{6,4},{7,5},{8,10},{9,11},{10,... | collective-permute-start | bytes 393224 | tf_op jit(solution)/shard_map/ppermute | solution.py:258
  18.4 1.9 %collective-permute-done.3 = bf16[32,2048]{1,0:T(8,128)(2,1)S(1)} collective-permute-done((bf16[32,2048]{1,0:T(8,128)(2,1)S(1)}, bf16[32,2048]{1,0:T(8,128)(2,1)S(1)}, u32[]{:S(2)}, u32[]{:S(2)}) %collective-permute-start.3) | collective-permute-done | bytes 131104 | tf_op jit(solution)/shard_map/ppermute | solution.py:258
  20.5 3.0 %collective-permute-start.9 = (bf16[8,4096]{1,0:T(8,128)(2,1)S(1)}, bf16[8,4096]{1,0:T(8,128)(2,1)S(1)}, u32[]{:S(2)}, u32[]{:S(2)}) collective-permute-start(bf16[8,4096]{1,0:T(8,128)(2,1)S(1)} %broadcast_add_fusion.3), channel_id=1, source_target_pairs={{0,12},{1,13},{2,14},{3,15},{4,8},{5,9},{6,10},{7,11},{8,4},{9,5},... | collective-permute-start | bytes 196616 | tf_op jit(solution)/shard_map/ppermute | solution.py:258
  25.5 1.6 %collective-permute-start.6 = (bf16[64,2176]{1,0:T(8,128)(2,1)S(1)}, bf16[64,2176]{1,0:T(8,128)(2,1)S(1)}, u32[]{:S(2)}, u32[]{:S(2)}) collective-permute-start(bf16[64,2176]{1,0:T(8,128)(2,1)S(1)} %get-tuple-element.37), channel_id=1, source_target_pairs={{0,2},{1,3},{2,0},{3,1},{4,6},{5,7},{6,4},{7,5},{8,10},{9,11},{10,... | collective-permute-start | bytes 835592 | tf_op jit(solution)/shard_map/ppermute | solution.py:258
  27.1 1.7 %collective-permute-done.8 = bf16[8,4096]{1,0:T(8,128)(2,1)S(1)} collective-permute-done((bf16[8,4096]{1,0:T(8,128)(2,1)S(1)}, bf16[8,4096]{1,0:T(8,128)(2,1)S(1)}, u32[]{:S(2)}, u32[]{:S(2)}) %collective-permute-start.8) | collective-permute-done | bytes 65568 | tf_op jit(solution)/shard_map/ppermute | solution.py:258
  30.4 1.7 %collective-permute-done.6 = bf16[64,2176]{1,0:T(8,128)(2,1)S(1)} collective-permute-done((bf16[64,2176]{1,0:T(8,128)(2,1)S(1)}, bf16[64,2176]{1,0:T(8,128)(2,1)S(1)}, u32[]{:S(2)}, u32[]{:S(2)}) %collective-permute-start.6) | collective-permute-done | bytes 278560 | tf_op jit(solution)/shard_map/ppermute | solution.py:258
  40.0 1.7 %collective-permute-done.11 = bf16[32,2048]{1,0:T(8,128)(2,1)S(1)} collective-permute-done((bf16[32,2048]{1,0:T(8,128)(2,1)S(1)}, bf16[32,2048]{1,0:T(8,128)(2,1)S(1)}, u32[]{:S(2)}, u32[]{:S(2)}) %collective-permute-start.11) | collective-permute-done | bytes 131104 | tf_op jit(solution)/shard_map/ppermute | solution.py:258
  43.2 4.0 %hidden.1 = (bf16[384,256]{1,0:T(8,128)(2,1)S(1)}, f32[384,256]{1,0:T(8,128)S(1)}, f32[384,256]{1,0:T(8,128)S(1)}, bf16[16,2048]{1,0:T(8,128)(2,1)S(1)}) custom-call(bf16[128,4224]{1,0:T(8,128)(2,1)S(1)} %pad_maximum_fusion.xa.ra, bf16[128,4224]{1,0:T(8,128)(2,1)S(1)} %collective-permute-done.7.xb.rb, bf16[768,4096]{1,0:T(8,128)(2,1)S(1)} %stage_in.1.win, ...), custom_call_target="tpu_custom_call" | custom-call | flops 1610612736 | bytes 10485760 | tf_op jit(solution)/shard_map/hidden/pallas_call | solution.py:389
  48.9 2.1 %part.1 = (bf16[128,2048]{1,0:T(8,128)(2,1)S(1)}, bf16[128,2048]{1,0:T(8,128)(2,1)S(1)}, bf16[128,4096]{1,0:T(8,128)(2,1)S(1)}, f32[256,128]{1,0:T(8,128)S(1)}, f32[256,128]{1,0:T(8,128)S(1)}) custom-call(s32[16]{0:T(128)S(1)} %copy-done.1, bf16[128,4224]{1,0:T(8,128)(2,1)S(1)} %pad_maximum_fusion.xa.ra, bf16[128,4224]{1,0:T(8,128)(2,1)S(1)} %collective-permute-done.7.xb.rb, ...), custom_call_target="tpu_custom_call" | custom-call | flops 805306368 | bytes 5242880 | tf_op jit(solution)/shard_map/part/pallas_call | solution.py:411
  51.2 2.5 %collective-permute-start.33 = (bf16[384,256]{1,0:T(8,128)(2,1)S(1)}, bf16[384,256]{1,0:T(8,128)(2,1)S(1)}, u32[]{:S(2)}, u32[]{:S(2)}) collective-permute-start(bf16[384,256]{1,0:T(8,128)(2,1)S(1)} %get-tuple-element.16.act.own), channel_id=1, source_target_pairs={{0,8},{1,9},{2,10},{3,11},{4,12},{5,13},{6,14},{7,15},{8,0},{9,1},... | collective-permute-start | bytes 589832 | tf_op jit(solution)/shard_map/ppermute | solution.py:258
  53.7 2.7 %factors.1.grad.own = bf16[768,256]{1,0:T(8,128)(2,1)S(1)} custom-call(bf16[128,4096]{1,0:T(8,128)(2,1)S(1)} %pad_maximum_fusion.1.after.ya.ra, bf16[128,4096]{1,0:T(8,128)(2,1)S(1)} %collective-permute-done.17.yb.rb, f32[384,256]{1,0:T(8,128)S(1)} %get-tuple-element.20.silu, f32[384,256]{1,0:T(8,128)S(1)} %get-tuple-element.21.slope, ...), custom_call_target="tpu_custom_call" | custom-call | flops 805306368 | bytes 5242880 | tf_op jit(solution)/shard_map/factors/pallas_call | solution.py:425
  56.8 1.8 %back.1 = (bf16[128,2048]{1,0:T(8,128)(2,1)S(1)}, bf16[128,2048]{1,0:T(8,128)(2,1)S(1)}, bf16[128,4096]{1,0:T(8,128)(2,1)S(1)}) custom-call(bf16[768,256]{1,0:T(8,128)(2,1)S(1)} %factors.1.grad.own, bf16[768,4096]{1,0:T(8,128)(2,1)S(1)} %stage_in.1.win), custom_call_target="tpu_custom_call" | custom-call | flops 1610612736 | bytes 10485760 | tf_op jit(solution)/shard_map/back/pallas_call | solution.py:440
  59.0 1.6 %collective-permute-start.22 = (bf16[64,2048]{1,0:T(8,128)(2,1)S(1)}, bf16[64,2048]{1,0:T(8,128)(2,1)S(1)}, u32[]{:S(2)}, u32[]{:S(2)}) collective-permute-start(bf16[64,2048]{1,0:T(8,128)(2,1)S(1)} %bitcast.143), channel_id=1, source_target_pairs={{0,2},{1,3},{2,0},{3,1},{4,6},{5,7},{6,4},{7,5},{8,10},{9,11},{10,... | collective-permute-start | bytes 786440 | tf_op jit(solution)/shard_map/ppermute | solution.py:258
  63.4 4.7 %collective-permute-done.22 = bf16[64,2048]{1,0:T(8,128)(2,1)S(1)} collective-permute-done((bf16[64,2048]{1,0:T(8,128)(2,1)S(1)}, bf16[64,2048]{1,0:T(8,128)(2,1)S(1)}, u32[]{:S(2)}, u32[]{:S(2)}) %collective-permute-start.22) | collective-permute-done | bytes 262176 | tf_op jit(solution)/shard_map/ppermute | solution.py:258
  69.7 1.6 %collective-permute-start.19 = (bf16[32,2048]{1,0:T(8,128)(2,1)S(1)}, bf16[32,2048]{1,0:T(8,128)(2,1)S(1)}, u32[]{:S(2)}, u32[]{:S(2)}) collective-permute-start(bf16[32,2048]{1,0:T(8,128)(2,1)S(1)} %fusion.9), channel_id=1, source_target_pairs={{0,2},{1,3},{2,0},{3,1},{4,6},{5,7},{6,4},{7,5},{8,10},{9,11},{10,... | collective-permute-start | bytes 393224 | tf_op jit(solution)/shard_map/ppermute | solution.py:258
  71.3 2.4 %collective-permute-done.21 = bf16[64,2048]{1,0:T(8,128)(2,1)S(1)} collective-permute-done((bf16[64,2048]{1,0:T(8,128)(2,1)S(1)}, bf16[64,2048]{1,0:T(8,128)(2,1)S(1)}, u32[]{:S(2)}, u32[]{:S(2)}) %collective-permute-start.21) | collective-permute-done | bytes 262176 | tf_op jit(solution)/shard_map/ppermute | solution.py:258
  76.1 2.6 %collective-permute-done.23 = bf16[32,2048]{1,0:T(8,128)(2,1)S(1)} collective-permute-done((bf16[32,2048]{1,0:T(8,128)(2,1)S(1)}, bf16[32,2048]{1,0:T(8,128)(2,1)S(1)}, u32[]{:S(2)}, u32[]{:S(2)}) %collective-permute-start.23) | collective-permute-done | bytes 131104 | tf_op jit(solution)/shard_map/ppermute | solution.py:258
  81.5 1.8 %collective-permute-start.26 = (bf16[8,4096]{1,0:T(8,128)(2,1)S(1)}, bf16[8,4096]{1,0:T(8,128)(2,1)S(1)}, u32[]{:S(2)}, u32[]{:S(2)}) collective-permute-start(bf16[8,4096]{1,0:T(8,128)(2,1)S(1)} %get-tuple-element.53.refs_2_), channel_id=1, source_target_pairs={{0,12},{1,13},{2,14},{3,15},{4,8},{5,9},{6,10},{7,11},{8,4},{9,5},... | collective-permute-start | bytes 196616 | tf_op jit(solution)/shard_map/ppermute | solution.py:258
  88.5 1.8 %collective-permute-done.27 = bf16[32,2048]{1,0:T(8,128)(2,1)S(1)} collective-permute-done((bf16[32,2048]{1,0:T(8,128)(2,1)S(1)}, bf16[32,2048]{1,0:T(8,128)(2,1)S(1)}, u32[]{:S(2)}, u32[]{:S(2)}) %collective-permute-start.27) | collective-permute-done | bytes 131104 | tf_op jit(solution)/shard_map/ppermute | solution.py:258
  91.7 2.4 %collective-permute-start.30 = (bf16[8,4096]{1,0:T(8,128)(2,1)S(1)}, bf16[8,4096]{1,0:T(8,128)(2,1)S(1)}, u32[]{:S(2)}, u32[]{:S(2)}) collective-permute-start(bf16[8,4096]{1,0:T(8,128)(2,1)S(1)} %get-tuple-element.50.rest_1_), channel_id=1, source_target_pairs={{0,8},{1,9},{2,10},{3,11},{4,12},{5,13},{6,14},{7,15},{8,0},{9,1},... | collective-permute-start | bytes 196616 | tf_op jit(solution)/shard_map/ppermute | solution.py:258
  94.9 3.9 %grad_down.1 = bf16[1,384,4096]{2,1,0:T(8,128)(2,1)} custom-call(s32[16]{0:T(128)S(1)} %copy-done.1, bf16[384,256]{1,0:T(8,128)(2,1)S(1)} %get-tuple-element.16.act.own, bf16[384,256]{1,0:T(8,128)(2,1)S(1)} %collective-permute-done.33.away, f32[256,128]{1,0:T(8,128)S(1)} %get-tuple-element.27.gate, bf16[128,4096]{1,0:T(8,128)(2,1)S(1)} %pad_maximum_fusion.1.after.ya.ra, ...), custom_call_target="tpu_custom_call" | custom-call | flops 805306368 | bytes 5242880 | tf_op jit(solution)/shard_map/grad_down/pallas_call | solution.py:519
  98.8 4.3 %grad_in.1 = bf16[2,384,4096]{2,1,0:T(8,128)(2,1)} custom-call(s32[16]{0:T(128)S(1)} %copy-done.1, bf16[768,256]{1,0:T(8,128)(2,1)S(1)} %factors.1.grad.own, bf16[768,256]{1,0:T(8,128)(2,1)S(1)} %collective-permute-done.32.away, f32[256,128]{1,0:T(8,128)S(1)} %get-tuple-element.27.gate, bf16[128,4224]{1,0:T(8,128)(2,1)S(1)} %pad_maximum_fusion.xa.ra, ...), custom_call_target="tpu_custom_call" | custom-call | flops 1610612736 | bytes 8388608 | tf_op jit(solution)/shard_map/grad_in/pallas_call | solution.py:519
  (121 shorter events, 40.7 us)
Async XLA Ops:
  2.4 7.1 %collective-permute-start = (bf16[8,4224]{1,0:T(8,128)(2,1)S(1)}, bf16[8,4224]{1,0:T(8,128)(2,1)S(1)}, u32[]{:S(2)}, u32[]{:S(2)}) collective-permute-start(bf16[8,4224]{1,0:T(8,128)(2,1)S(1)} %pad_maximum_fusion.13), channel_id=1, source_target_pairs={{0,8},{1,9},{2,10},{3,11},{4,12},{5,13},{6,14},{7,15},{8,0},{9,1},... | collective-permute-start | bytes 202760 | tf_op jit(solution)/shard_map/ppermute | solution.py:258
  6.4 7.7 %collective-permute-start.2 = (bf16[8,4224]{1,0:T(8,128)(2,1)S(1)}, bf16[8,4224]{1,0:T(8,128)(2,1)S(1)}, u32[]{:S(2)}, u32[]{:S(2)}) collective-permute-start(bf16[8,4224]{1,0:T(8,128)(2,1)S(1)} %pad_maximum_fusion.13), channel_id=1, source_target_pairs={{0,4},{1,5},{2,6},{3,7},{4,0},{5,1},{6,2},{7,3},{8,12},{9,13},{10,... | collective-permute-start | bytes 202760 | tf_op jit(solution)/shard_map/ppermute | solution.py:258
  8.0 6.1 %collective-permute-start.1 = (bf16[8,4224]{1,0:T(8,128)(2,1)S(1)}, bf16[8,4224]{1,0:T(8,128)(2,1)S(1)}, u32[]{:S(2)}, u32[]{:S(2)}) collective-permute-start(bf16[8,4224]{1,0:T(8,128)(2,1)S(1)} %pad_maximum_fusion.13), channel_id=1, source_target_pairs={{0,12},{1,13},{2,14},{3,15},{4,8},{5,9},{6,10},{7,11},{8,4},{9,5},... | collective-permute-start | bytes 202760 | tf_op jit(solution)/shard_map/ppermute | solution.py:258
  16.8 8.6 %collective-permute-start.5 = (bf16[32,2176]{1,0:T(8,128)(2,1)S(1)}, bf16[32,2176]{1,0:T(8,128)(2,1)S(1)}, u32[]{:S(2)}, u32[]{:S(2)}) collective-permute-start(bf16[32,2176]{1,0:T(8,128)(2,1)S(1)} %pad_maximum_fusion.6), channel_id=1, source_target_pairs={{0,16},{16,0},{1,17},{17,1},{2,18},{18,2},{3,19},{19,3},{4,20},{20... | collective-permute-start | bytes 417800 | tf_op jit(solution)/shard_map/ppermute | solution.py:258
  20.4 11.9 %collective-permute-start.10 = (bf16[8,4096]{1,0:T(8,128)(2,1)S(1)}, bf16[8,4096]{1,0:T(8,128)(2,1)S(1)}, u32[]{:S(2)}, u32[]{:S(2)}) collective-permute-start(bf16[8,4096]{1,0:T(8,128)(2,1)S(1)} %broadcast_add_fusion.3), channel_id=1, source_target_pairs={{0,4},{1,5},{2,6},{3,7},{4,0},{5,1},{6,2},{7,3},{8,12},{9,13},{10,... | collective-permute-start | bytes 196616 | tf_op jit(solution)/shard_map/ppermute | solution.py:258
  20.5 8.3 %collective-permute-start.9 = (bf16[8,4096]{1,0:T(8,128)(2,1)S(1)}, bf16[8,4096]{1,0:T(8,128)(2,1)S(1)}, u32[]{:S(2)}, u32[]{:S(2)}) collective-permute-start(bf16[8,4096]{1,0:T(8,128)(2,1)S(1)} %broadcast_add_fusion.3), channel_id=1, source_target_pairs={{0,12},{1,13},{2,14},{3,15},{4,8},{5,9},{6,10},{7,11},{8,4},{9,5},... | collective-permute-start | bytes 196616 | tf_op jit(solution)/shard_map/ppermute | solution.py:258
  23.9 6.4 %collective-permute-start.4 = (bf16[64,2048]{1,0:T(8,128)(2,1)S(1)}, bf16[64,2048]{1,0:T(8,128)(2,1)S(1)}, u32[]{:S(2)}, u32[]{:S(2)}) collective-permute-start(bf16[64,2048]{1,0:T(8,128)(2,1)S(1)} %maximum_bitcast_fusion.2.refs_0_), channel_id=1, source_target_pairs={{0,16},{16,0},{1,17},{17,1},{2,18},{18,2},{3,19},{19,3},{4,20},{20... | collective-permute-start | bytes 786440 | tf_op jit(solution)/shard_map/ppermute | solution.py:258
  25.5 6.6 %collective-permute-start.6 = (bf16[64,2176]{1,0:T(8,128)(2,1)S(1)}, bf16[64,2176]{1,0:T(8,128)(2,1)S(1)}, u32[]{:S(2)}, u32[]{:S(2)}) collective-permute-start(bf16[64,2176]{1,0:T(8,128)(2,1)S(1)} %get-tuple-element.37), channel_id=1, source_target_pairs={{0,2},{1,3},{2,0},{3,1},{4,6},{5,7},{6,4},{7,5},{8,10},{9,11},{10,... | collective-permute-start | bytes 835592 | tf_op jit(solution)/shard_map/ppermute | solution.py:258
  32.2 10.9 %collective-permute-start.7 = (bf16[128,4224]{1,0:T(8,128)(2,1)S(1)}, bf16[128,4224]{1,0:T(8,128)(2,1)S(1)}, u32[]{:S(2)}, u32[]{:S(2)}) collective-permute-start(bf16[128,4224]{1,0:T(8,128)(2,1)S(1)} %pad_maximum_fusion.xa.ra), channel_id=1, source_target_pairs={{0,1},{1,0},{2,3},{3,2},{4,5},{5,4},{6,7},{7,6},{8,9},{9,8},{10,11... | collective-permute-start | bytes 3244040 | tf_op jit(solution)/shard_map/ppermute | solution.py:258
  32.4 6.0 %collective-permute-start.13 = (bf16[32,2048]{1,0:T(8,128)(2,1)S(1)}, bf16[32,2048]{1,0:T(8,128)(2,1)S(1)}, u32[]{:S(2)}, u32[]{:S(2)}) collective-permute-start(bf16[32,2048]{1,0:T(8,128)(2,1)S(1)} %get-tuple-element.45), channel_id=1, source_target_pairs={{0,16},{16,0},{1,17},{17,1},{2,18},{18,2},{3,19},{19,3},{4,20},{20... | collective-permute-start | bytes 393224 | tf_op jit(solution)/shard_map/ppermute | solution.py:258
  38.4 8.8 %collective-permute-start.14 = (bf16[64,2048]{1,0:T(8,128)(2,1)S(1)}, bf16[64,2048]{1,0:T(8,128)(2,1)S(1)}, u32[]{:S(2)}, u32[]{:S(2)}) collective-permute-start(bf16[64,2048]{1,0:T(8,128)(2,1)S(1)} %get-tuple-element.47), channel_id=1, source_target_pairs={{0,2},{1,3},{2,0},{3,1},{4,6},{5,7},{6,4},{7,5},{8,10},{9,11},{10,... | collective-permute-start | bytes 786440 | tf_op jit(solution)/shard_map/ppermute | solution.py:258
  41.7 6.4 %collective-permute-start.12 = (bf16[64,2048]{1,0:T(8,128)(2,1)S(1)}, bf16[64,2048]{1,0:T(8,128)(2,1)S(1)}, u32[]{:S(2)}, u32[]{:S(2)}) collective-permute-start(bf16[64,2048]{1,0:T(8,128)(2,1)S(1)} %maximum_bitcast_fusion.3), channel_id=1, source_target_pairs={{0,16},{16,0},{1,17},{17,1},{2,18},{18,2},{3,19},{19,3},{4,20},{20... | collective-permute-start | bytes 786440 | tf_op jit(solution)/shard_map/ppermute | solution.py:258
  51.0 7.8 %collective-permute-start.15 = (bf16[128,4096]{1,0:T(8,128)(2,1)S(1)}, bf16[128,4096]{1,0:T(8,128)(2,1)S(1)}, u32[]{:S(2)}, u32[]{:S(2)}) collective-permute-start(bf16[128,4096]{1,0:T(8,128)(2,1)S(1)} %get-tuple-element.19.after), channel_id=1, source_target_pairs={{0,1},{1,0},{2,3},{3,2},{4,5},{5,4},{6,7},{7,6},{8,9},{9,8},{10,11... | collective-permute-start | bytes 3145736 | tf_op jit(solution)/shard_map/ppermute | solution.py:258
  51.2 43.7 %collective-permute-start.33 = (bf16[384,256]{1,0:T(8,128)(2,1)S(1)}, bf16[384,256]{1,0:T(8,128)(2,1)S(1)}, u32[]{:S(2)}, u32[]{:S(2)}) collective-permute-start(bf16[384,256]{1,0:T(8,128)(2,1)S(1)} %get-tuple-element.16.act.own), channel_id=1, source_target_pairs={{0,8},{1,9},{2,10},{3,11},{4,12},{5,13},{6,14},{7,15},{8,0},{9,1},... | collective-permute-start | bytes 589832 | tf_op jit(solution)/shard_map/ppermute | solution.py:258
  56.3 42.4 %collective-permute-start.32 = (bf16[768,256]{1,0:T(8,128)(2,1)S(1)}, bf16[768,256]{1,0:T(8,128)(2,1)S(1)}, u32[]{:S(2)}, u32[]{:S(2)}) collective-permute-start(bf16[768,256]{1,0:T(8,128)(2,1)S(1)} %factors.1.grad.own), channel_id=1, source_target_pairs={{0,8},{1,9},{2,10},{3,11},{4,12},{5,13},{6,14},{7,15},{8,0},{9,1},... | collective-permute-start | bytes 1179656 | tf_op jit(solution)/shard_map/ppermute | solution.py:258
  59.0 9.2 %collective-permute-start.22 = (bf16[64,2048]{1,0:T(8,128)(2,1)S(1)}, bf16[64,2048]{1,0:T(8,128)(2,1)S(1)}, u32[]{:S(2)}, u32[]{:S(2)}) collective-permute-start(bf16[64,2048]{1,0:T(8,128)(2,1)S(1)} %bitcast.143), channel_id=1, source_target_pairs={{0,2},{1,3},{2,0},{3,1},{4,6},{5,7},{6,4},{7,5},{8,10},{9,11},{10,... | collective-permute-start | bytes 786440 | tf_op jit(solution)/shard_map/ppermute | solution.py:258
  60.7 8.9 %collective-permute-start.16 = (bf16[64,2048]{1,0:T(8,128)(2,1)S(1)}, bf16[64,2048]{1,0:T(8,128)(2,1)S(1)}, u32[]{:S(2)}, u32[]{:S(2)}) collective-permute-start(bf16[64,2048]{1,0:T(8,128)(2,1)S(1)} %get-tuple-element.29), channel_id=1, source_target_pairs={{0,16},{16,0},{1,17},{17,1},{2,18},{18,2},{3,19},{19,3},{4,20},{20... | collective-permute-start | bytes 786440 | tf_op jit(solution)/shard_map/ppermute | solution.py:258
  62.5 11.2 %collective-permute-start.21 = (bf16[64,2048]{1,0:T(8,128)(2,1)S(1)}, bf16[64,2048]{1,0:T(8,128)(2,1)S(1)}, u32[]{:S(2)}, u32[]{:S(2)}) collective-permute-start(bf16[64,2048]{1,0:T(8,128)(2,1)S(1)} %bitcast.104), channel_id=1, source_target_pairs={{0,2},{1,3},{2,0},{3,1},{4,6},{5,7},{6,4},{7,5},{8,10},{9,11},{10,... | collective-permute-start | bytes 786440 | tf_op jit(solution)/shard_map/ppermute | solution.py:258
  68.1 7.5 %collective-permute-start.20 = (bf16[64,2048]{1,0:T(8,128)(2,1)S(1)}, bf16[64,2048]{1,0:T(8,128)(2,1)S(1)}, u32[]{:S(2)}, u32[]{:S(2)}) collective-permute-start(bf16[64,2048]{1,0:T(8,128)(2,1)S(1)} %get-tuple-element.33.refs_0_), channel_id=1, source_target_pairs={{0,16},{16,0},{1,17},{17,1},{2,18},{18,2},{3,19},{19,3},{4,20},{20... | collective-permute-start | bytes 786440 | tf_op jit(solution)/shard_map/ppermute | solution.py:258
  69.7 6.5 %collective-permute-start.19 = (bf16[32,2048]{1,0:T(8,128)(2,1)S(1)}, bf16[32,2048]{1,0:T(8,128)(2,1)S(1)}, u32[]{:S(2)}, u32[]{:S(2)}) collective-permute-start(bf16[32,2048]{1,0:T(8,128)(2,1)S(1)} %fusion.9), channel_id=1, source_target_pairs={{0,2},{1,3},{2,0},{3,1},{4,6},{5,7},{6,4},{7,5},{8,10},{9,11},{10,... | collective-permute-start | bytes 393224 | tf_op jit(solution)/shard_map/ppermute | solution.py:258
  81.5 6.2 %collective-permute-start.26 = (bf16[8,4096]{1,0:T(8,128)(2,1)S(1)}, bf16[8,4096]{1,0:T(8,128)(2,1)S(1)}, u32[]{:S(2)}, u32[]{:S(2)}) collective-permute-start(bf16[8,4096]{1,0:T(8,128)(2,1)S(1)} %get-tuple-element.53.refs_2_), channel_id=1, source_target_pairs={{0,12},{1,13},{2,14},{3,15},{4,8},{5,9},{6,10},{7,11},{8,4},{9,5},... | collective-permute-start | bytes 196616 | tf_op jit(solution)/shard_map/ppermute | solution.py:258
  90.4 8.3 %collective-permute-start.29 = (bf16[8,4096]{1,0:T(8,128)(2,1)S(1)}, bf16[8,4096]{1,0:T(8,128)(2,1)S(1)}, u32[]{:S(2)}, u32[]{:S(2)}) collective-permute-start(bf16[8,4096]{1,0:T(8,128)(2,1)S(1)} %slice.280.rest_0_), channel_id=1, source_target_pairs={{0,4},{1,5},{2,6},{3,7},{4,0},{5,1},{6,2},{7,3},{8,12},{9,13},{10,... | collective-permute-start | bytes 196616 | tf_op jit(solution)/shard_map/ppermute | solution.py:258
  91.7 11.4 %collective-permute-start.30 = (bf16[8,4096]{1,0:T(8,128)(2,1)S(1)}, bf16[8,4096]{1,0:T(8,128)(2,1)S(1)}, u32[]{:S(2)}, u32[]{:S(2)}) collective-permute-start(bf16[8,4096]{1,0:T(8,128)(2,1)S(1)} %get-tuple-element.50.rest_1_), channel_id=1, source_target_pairs={{0,8},{1,9},{2,10},{3,11},{4,12},{5,13},{6,14},{7,15},{8,0},{9,1},... | collective-permute-start | bytes 196616 | tf_op jit(solution)/shard_map/ppermute | solution.py:258
  94.1 9.0 %collective-permute-start.31 = (bf16[8,4096]{1,0:T(8,128)(2,1)S(1)}, bf16[8,4096]{1,0:T(8,128)(2,1)S(1)}, u32[]{:S(2)}, u32[]{:S(2)}) collective-permute-start(bf16[8,4096]{1,0:T(8,128)(2,1)S(1)} %get-tuple-element.51.rest_2_), channel_id=1, source_target_pairs={{0,12},{1,13},{2,14},{3,15},{4,8},{5,9},{6,10},{7,11},{8,4},{9,5},... | collective-permute-start | bytes 196616 | tf_op jit(solution)/shard_map/ppermute | solution.py:258
  (15 other events, 94.4 us)
where the time goes:
time: 104 us
  starting transfers between devices  44.3 us (43%)
  waiting for transfers between devices  29.8 us (29%)
  Pallas kernels  20.8 us (20%)
  other arithmetic  5.83 us (6%)
  local copies, waits for them, and re-layouts  1.96 us (2%)
  between operations  1.16 us (1%)
    ppermute x34, starting transfers between devices, partner(): lax.ppermute(block, axis, [(i, i ^ mask) for i in range(lax.axis_size(axi...  44.3 us
    ppermute x34, waiting for transfers between devices, partner(): lax.ppermute(block, axis, [(i, i ^ mask) for i in range(lax.axis_size(axi...  29.8 us
    pallas_call x2, Pallas kernels, weight_gradient(): pl.pallas_call(functools.partial(weight_kernel, scaled), out_shape=jax.Sh...  8.2 us
    pallas_call x1, Pallas kernels, on_device(): pl.pallas_call(hidden_kernel, out_shape=[jax.ShapeDtypeStruct((units, row...  4.01 us
    pallas_call x1, Pallas kernels, on_device(): pl.pallas_call(factor_kernel, out_shape=jax.ShapeDtypeStruct((2 * units,...  2.65 us
    pallas_call x1, Pallas kernels, on_device(): pl.pallas_call(functools.partial(part_kernel, experts), out_shape=[*rows_...  2.09 us
  transfers between devices with their start and end apart: 34, of which 18 were waited for; matrix products, arithmetic and copies ran while one was open for 2% of the time, Pallas kernels for 20%

commit v1 on v0

v1 whole, which is shorter than its diff:
```python
import functools

import jax
import jax.numpy as jnp
from jax import lax
from jax.experimental import pallas as pl
from jax.experimental.pallas import tpu as pltpu
from jax.sharding import PartitionSpec as P

F32, BF16 = jnp.float32, jnp.bfloat16
ANY = pl.BlockSpec(memory_space=pl.ANY)
SMEM = pl.BlockSpec(memory_space=pltpu.SMEM)
VMEM = pl.BlockSpec(memory_space=pltpu.VMEM)
CHUNKS = 4
ROW_BLOCK = 256
STAGE_MIB = 40


def nt(a, b):
    return lax.dot_general(a, b, (((1,), (1,)), ((), ())), preferred_element_type=F32)


def nn(a, b):
    return jnp.dot(a, b, preferred_element_type=F32)


def each_rows(total, body):
    if total <= ROW_BLOCK:
        body(pl.ds(0, total))
    else:

        @pl.loop(0, total // ROW_BLOCK)
        def _(i):
            body(pl.ds(pl.multiple_of(i * ROW_BLOCK, ROW_BLOCK), ROW_BLOCK))


def columns(dim):
    step = dim // CHUNKS
    return [pl.ds(c * step, step) for c in range(CHUNKS)]


def started(sems, base, pairs):
    copies = [
        pltpu.make_async_copy(source, target, sems.at[base + i])
        for i, (source, target) in enumerate(pairs)
    ]
    for copy in copies:
        copy.start()
    return copies


def wait(copies):
    for copy in copies:
        copy.wait()


def row_copies(own, received, buffer, cols, target=None):
    half = own.shape[0]
    target = cols if target is None else target
    return [
        (own.at[:, cols], buffer.at[pl.ds(0, half), target]),
        (received.at[:, cols], buffer.at[pl.ds(half, half), target]),
    ]


def split_three(x):
    high = x.astype(BF16)
    rest = x - high.astype(F32)
    middle = rest.astype(BF16)
    low = (rest - middle.astype(F32)).astype(BF16)
    return high, middle, low


def gate_column(parts, expert, experts):
    lane = lax.broadcasted_iota(jnp.int32, parts.shape, 1)
    values = parts.astype(F32)
    high, middle, low = (
        jnp.sum(jnp.where(lane == expert + i * experts, values, 0.0), axis=1, keepdims=True)
        for i in range(3)
    )
    return (low + middle) + high


def fill_gates(parts, gate, expert, experts):
    def body(rows):
        column = gate_column(parts[rows, :], expert, experts)
        gate[rows, :] = jnp.broadcast_to(column, (column.shape[0], gate.shape[1]))

    each_rows(parts.shape[0], body)


def held_expert(flags):
    me = lax.axis_index("expert")
    flag = flags[me]
    return me, jnp.where(flag > 0, me ^ (lax.axis_size("expert") // 2), me), flag


def stage_kernel(after, weight, out, sems):
    wait(started(sems, 0, [(weight.at[:, c], out.at[:, c]) for c in columns(weight.shape[1])]))


def zero_kernel(*refs):
    refs[-1][...] = jnp.zeros_like(refs[-1])


def hidden_kernel(xa, xb, win, after, act, silu, slope, x, hidden, sems):
    units, rows_all = act.shape
    dim = win.shape[1]
    loads = []
    for c, cols in enumerate(columns(dim)):
        loads.append(started(sems, 2 * c, row_copies(xa, xb, x, cols)))
    for c, cols in enumerate(columns(dim)):
        wait(loads[c])

        def multiply(rows):
            product = nt(win[:, cols], x[rows, cols])
            hidden[:, rows] = product if c == 0 else hidden[:, rows] + product

        each_rows(rows_all, multiply)

    def pointwise(rows):
        g, u = hidden[pl.ds(0, units), rows], hidden[pl.ds(units, units), rows]
        sig = jax.nn.sigmoid(g)
        gated = g * sig
        silu[:, rows] = gated
        slope[:, rows] = u * sig * (1.0 + g * (1.0 - sig))
        act[:, rows] = (gated * u).astype(BF16)

    each_rows(rows_all, pointwise)


def split_product(rows_ref, weight, keep, send, cols, to, finish):
    half = send.shape[0]

    def multiply(start, target, place):
        def body(rows):
            mine = pl.ds(rows.start + start, rows.size)
            target[rows, place] = finish(mine, nn(rows_ref[mine, :], weight[:, cols]).astype(BF16))

        return body

    each_rows(half, multiply(half, send, to))
    each_rows(half, multiply(0, keep, cols))


def output_kernel(
    gate, factors, win, wdown, mixed, back, send, rows_act, rows_grad
):
    units, dim = wdown.shape

    def turn(rows):
        rows_act[rows, :] = factors[pl.ds(0, units), rows].T
        rows_grad[rows, :] = factors[pl.ds(units, 2 * units), rows].T

    def weighted(rows, part):
        return (gate[rows, pl.ds(0, 1)] * part.astype(F32)).astype(BF16)

    each_rows(rows_act.shape[0], turn)
    for cols in columns(dim):
        split_product(rows_act, wdown, mixed, send, cols, cols, weighted)
    for cols in columns(dim):
        to = pl.ds(dim + cols.start, cols.size)
        split_product(rows_grad, win, back, send, cols, to, lambda rows, part: part)


def factor_kernel(
    experts, flags, xa, xb, ya, yb, act, silu, slope, wdown, factors, gate, gate_held,
    y, total, parts, sems,
):
    units, dim = wdown.shape
    rows_all, width = parts.shape
    loads = []
    gates = started(sems, 0, row_copies(xa, xb, parts, pl.ds(dim, width), pl.ds(0, width)))
    for c, cols in enumerate(columns(dim)):
        loads.append(started(sems, 2 + 2 * c, row_copies(ya, yb, y, cols)))
    factors[pl.ds(0, units), :] = act[...]
    me, held, _ = held_expert(flags)
    wait(gates)
    fill_gates(parts, gate, me, experts)
    for c, cols in enumerate(columns(dim)):
        wait(loads[c])

        def multiply(rows):
            scaled = (gate[rows, pl.ds(0, 1)] * y[rows, cols].astype(F32)).astype(BF16)
            product = nt(wdown[:, cols], scaled)
            total[:, rows] = product if c == 0 else total[:, rows] + product

        each_rows(rows_all, multiply)

    def pointwise(rows):
        value = total[:, rows]
        factors[pl.ds(units, units), rows] = (value * slope[:, rows]).astype(BF16)
        factors[pl.ds(2 * units, units), rows] = (value * silu[:, rows]).astype(BF16)

    each_rows(rows_all, pointwise)
    fill_gates(parts, gate_held, held, experts)


def weight_kernel(first, scaled, flags, own, away, gate, ra, rb, *rest):
    grads, r, used, out, sems = rest[-5:]
    groups, units, dim = grads.shape
    rows_all = r.shape[0]
    base, loads, stores = 0, [], []
    for cols in columns(dim):
        loads.append(started(sems, base, row_copies(ra, rb, r, cols)))
        base += 2
    _, _, flag = held_expert(flags)
    some = pl.ds(first * units, groups * units)
    used[...] = jnp.where(flag > 0, away[some, :], own[some, :])
    for c, cols in enumerate(columns(dim)):
        wait(loads[c])
        if scaled:

            def scale(rows):
                r[rows, cols] = (gate[rows, pl.ds(0, 1)] * r[rows, cols].astype(F32)).astype(BF16)

            each_rows(rows_all, scale)
        pairs = []
        for i in range(groups):
            some = pl.ds(i * units, units)
            out[some, cols] = nn(used[some, :], r[:, cols]).astype(BF16)
            pairs.append((out.at[some, cols], grads.at[i, :, cols]))
        stores.append(started(sems, base, pairs))
        base += groups
    for store in stores:
        wait(store)


def rounded_up(value, unit):
    return -(-value // unit) * unit


def params(mib):
    return pltpu.CompilerParams(vmem_limit_bytes=mib * 1024 * 1024)


def cost(flops, size):
    return pl.CostEstimate(flops=flops, bytes_accessed=size, transcendentals=0)


def masks(axis):
    size, out = lax.axis_size(axis), []
    while size > 1:
        size //= 2
        out.append((axis, size))
    return out


def partner(block, bit):
    axis, mask = bit
    return lax.ppermute(block, axis, [(i, i ^ mask) for i in range(lax.axis_size(axis))])


def inner_rows(bit, done, order, unit):
    for other in done:
        if order.index(other) > order.index(bit):
            unit *= 2
    return unit


def join(a, b, inner):
    pair = [part.reshape(-1, inner, part.shape[-1]) for part in (a, b)]
    return jnp.concatenate(pair, axis=1).reshape(-1, a.shape[-1])


def halves(block, inner):
    split = block.reshape(-1, 2, inner, block.shape[1])
    return [split[:, i].reshape(-1, block.shape[1]) for i in (0, 1)]


def is_set(bit):
    return (lax.axis_index(bit[0]) & bit[1]) > 0


def add(a, b):
    return (a.astype(F32) + b.astype(F32)).astype(BF16)


def on_device(tokens, cotangent, gates, expert_ids, swap_flag, w_in, w_down):
    experts = lax.axis_size("expert")
    half_axis = experts // 2
    tok_dev, dim = tokens.shape
    units = w_down.shape[1]

    across, within = masks("dp"), masks("expert")
    core, near, far = within[-1], within[-2:-1], within[:-2]
    first = near + across
    second = across + near
    order = first[::-1] + far[::-1]
    rows_all = tok_dev * lax.axis_size("dp") * experts
    top = far[0]

    slots = jnp.arange(experts, dtype=jnp.int32)
    dense = jnp.sum(
        jnp.where(expert_ids[:, :, None] == slots, gates[:, :, None], 0.0), axis=1
    )
    parts = jnp.concatenate(split_three(dense), axis=1)
    width = rounded_up(parts.shape[1], 128)
    parts = jnp.pad(parts, ((0, 0), (0, width - parts.shape[1])))
    payload = jnp.stack([jnp.concatenate([rows, parts], axis=1) for rows in (tokens, cotangent)])

    def far_gather(block, seen):
        for i in range(0, len(far), 2):
            group = far[i : i + 2]
            flat = block.reshape(-1, block.shape[2])

            def arrived(mask):
                return partner(flat, ("expert", mask)).reshape(block.shape)

            a = group[0]
            if len(group) == 2:
                b = group[1]
                fours = [block, arrived(b[1]), arrived(a[1]), arrived(a[1] | b[1])]
                seen.append(fours[1])
                pairs = [jnp.concatenate(fours[:2], axis=1), jnp.concatenate(fours[2:], axis=1)]
            else:
                pairs = [block, arrived(a[1])]
                seen.append(pairs[1])
            if a == top:
                turn = is_set(top)
                pairs = [jnp.where(turn, pairs[1 - j], pairs[j]) for j in (0, 1)]
            block = jnp.concatenate(pairs, axis=1)
        return block

    def plane(rows, route):
        far_rows = rows.shape[0]
        for k, bit in enumerate(route):
            rows = join(rows, partner(rows, bit), inner_rows(bit, route[:k], order, far_rows))
        return rows

    def stage(after, weight, name):
        return pl.pallas_call(
            stage_kernel,
            out_shape=jax.ShapeDtypeStruct(weight.shape, BF16),
            in_specs=[ANY] * 2,
            out_specs=VMEM,
            scratch_shapes=[pltpu.SemaphoreType.DMA((CHUNKS,))],
            compiler_params=params(STAGE_MIB),
            cost_estimate=cost(0, 4 * weight.size),
            name=name,
        )(after, weight)

    seen = []
    x_far, y_far = far_gather(payload, seen)
    win = stage(seen[0], w_in.reshape(2 * units, dim), "stage_in")
    wdown = stage(seen[0], w_down.reshape(units, dim), "stage_down")
    xa, ya = plane(x_far, first), plane(y_far, second)
    xb, yb = partner(xa, core), partner(ya, core)

    half_rows = rows_all // 2
    limit = 60 if rows_all > 512 else 24
    rows_out = [jax.ShapeDtypeStruct((half_rows, dim), BF16)] * 2
    gate_type = jax.ShapeDtypeStruct((rows_all, 128), F32)
    saved_type = jax.ShapeDtypeStruct((units, rows_all), F32)
    product = 2 * rows_all * units * dim
    act, silu, slope = pl.pallas_call(
        hidden_kernel,
        out_shape=[
            jax.ShapeDtypeStruct((units, rows_all), BF16),
            saved_type,
            saved_type,
        ],
        in_specs=[ANY, ANY, VMEM, ANY],
        out_specs=[VMEM] * 3,
        scratch_shapes=[
            pltpu.VMEM((rows_all, dim), BF16),
            pltpu.VMEM((2 * units, rows_all), F32),
            pltpu.SemaphoreType.DMA((2 * CHUNKS,)),
        ],
        compiler_params=params(limit),
        cost_estimate=cost(2 * product, 4 * dim * (units + rows_all)),
        name="hidden",
    )(xa, xb, win, wdown)
    factors, gate, gate_held = pl.pallas_call(
        functools.partial(factor_kernel, experts),
        out_shape=[jax.ShapeDtypeStruct((3 * units, rows_all), BF16), gate_type, gate_type],
        in_specs=[SMEM] + [ANY] * 4 + [VMEM] * 4,
        out_specs=[VMEM] * 3,
        scratch_shapes=[
            pltpu.VMEM((rows_all, dim), BF16),
            pltpu.VMEM((units, rows_all), F32),
            pltpu.VMEM((rows_all, width), BF16),
            pltpu.SemaphoreType.DMA((2 + 2 * CHUNKS,)),
        ],
        compiler_params=params(limit),
        cost_estimate=cost(product, 2 * dim * (units + rows_all)),
        name="factors",
    )(swap_flag, xa, xb, ya, yb, act, silu, slope, wdown)
    far_factors = partner(factors, ("expert", half_axis))
    mixed_keep, back_keep, send = pl.pallas_call(
        output_kernel,
        out_shape=[
            jax.ShapeDtypeStruct((half_rows, dim), BF16),
            jax.ShapeDtypeStruct((half_rows, dim), BF16),
            jax.ShapeDtypeStruct((half_rows, 2 * dim), BF16),
        ],
        in_specs=[VMEM] * 4,
        out_specs=[VMEM] * 3,
        scratch_shapes=[
            pltpu.VMEM((rows_all, units), BF16),
            pltpu.VMEM((rows_all, 2 * units), BF16),
        ],
        compiler_params=params(limit),
        cost_estimate=cost(3 * product, 6 * dim * (units + rows_all)),
        name="outputs",
    )(gate, factors, win, wdown)

    def added(keep, got, bit, left):
        inner = inner_rows(bit, left, order, tok_dev)
        return [add(*pair) for pair in zip(halves(keep, inner), halves(got, inner))]

    def far_sends(keep, groups):
        group = groups[-1]
        a = group[0]
        inner = keep.shape[0] // 2
        pair = [keep[:inner], keep[inner:]]
        if a == top:
            turn = is_set(top)
            pair = [jnp.where(turn, pair[1 - j], pair[j]) for j in (0, 1)]
        if len(group) == 1:
            return pair[0], [(pair[1], a[1])]
        b = group[1]
        low = inner // 2
        return pair[0][:low], [
            (pair[0][low:], b[1]),
            (pair[1][:low], a[1]),
            (pair[1][low:], a[1] | b[1]),
        ]

    def far_sum(mine, sends):
        arrived = [partner(rows, ("expert", mask)) for rows, mask in sends]
        total = mine.astype(F32)
        for rows in arrived:
            total = total + rows.astype(F32)
        return total.astype(BF16), arrived[0]

    groups = [far[i : i + 2] for i in range(0, len(far), 2)]

    def plane_step(keep, got, route, k):
        left = set(order) - set(route[: k + 1])
        keep, sent = added(keep, got, route[k], left)
        return keep, partner(sent, route[k]), sent

    def zero_after(*arrays):
        return pl.pallas_call(
            zero_kernel,
            out_shape=jax.ShapeDtypeStruct((16, dim), BF16),
            in_specs=[ANY] * len(arrays),
            out_specs=VMEM,
            compiler_params=params(2),
            name="zero",
        )(*arrays)[:1]

    def weight_gradient(after, first, groups, pieces, scaled, name):
        return pl.pallas_call(
            functools.partial(weight_kernel, first, scaled),
            out_shape=jax.ShapeDtypeStruct((groups, units, dim), BF16),
            in_specs=[SMEM] + [VMEM] * 3 + [ANY] * (2 + len(after)),
            out_specs=ANY,
            scratch_shapes=[
                pltpu.VMEM((rows_all, dim), BF16),
                pltpu.VMEM((groups * units, rows_all), BF16),
                pltpu.VMEM((groups * units, dim), BF16),
                pltpu.SemaphoreType.DMA(((2 + groups) * CHUNKS,)),
            ],
            compiler_params=params(limit),
            cost_estimate=cost(groups * product, 2 * dim * (groups * units + rows_all)),
            name=name,
        )(swap_flag, factors, far_factors, gate_held, *pieces, *after)

    across_first, near_first = first[::-1], second[::-1]
    got = partner(send, core)
    mixed_keep, mixed_got, mixed_sent = plane_step(mixed_keep, got[:, :dim], across_first, 0)
    back_keep, back_got, back_sent = plane_step(back_keep, got[:, dim:], near_first, 0)
    for k in range(1, len(first)):
        mixed_keep, mixed_got, mixed_sent = plane_step(mixed_keep, mixed_got, across_first, k)
        back_keep, back_got, back_sent = plane_step(back_keep, back_got, near_first, k)
    zero = zero_after(far_factors, mixed_sent, back_sent)
    both = jnp.concatenate(
        [add(mixed_keep, mixed_got + zero), add(back_keep, back_got + zero)], axis=1
    )
    for group in groups[::-1]:
        mine, sends = far_sends(both, [group])
        both, _ = far_sum(mine, sends)
    mixed, grad_tokens = both[:, :dim], both[:, dim:]
    behind = [rows for rows, _ in sends]
    new_down = weight_gradient(behind, 0, 1, (ya, yb), True, "grad_down")
    new_in = weight_gradient(behind, 1, 2, (xa, xb), False, "grad_in")
    return (mixed, grad_tokens, new_in.reshape(w_in.shape), new_down.reshape(w_down.shape))


def solution(mesh):
    rows = P(("dp", "expert"), None)
    w_in, w_down = P("expert", None, "dp", None), P("expert", "dp", None)
    return jax.shard_map(
        on_device,
        mesh=mesh,
        in_specs=(rows, rows, rows, rows, P(), w_in, w_down),
        out_specs=(rows, rows, w_in, w_down),
        check_vma=False,
    )
```

time: 104 us -> 102 us (0.981)
  starting transfers between devices: 44.3 us -> 22.3 us
  waiting for transfers between devices: 29.8 us -> 50 us
  other arithmetic: 5.83 us -> 3.22 us
  local copies, waits for them, and re-layouts: 1.96 us -> 4.4 us
    ppermute x34 -> x18, starting transfers between devices: 44.3 us -> 22.3 us  [partner(): lax.ppermute(block, axis, [(i, i ^ mask) for i in range(lax.axis_size(axi...]
    ppermute x34 -> x18, waiting for transfers between devices: 29.8 us -> 50 us  [partner(): lax.ppermute(block, axis, [(i, i ^ mask) for i in range(lax.axis_size(axi...]
    unnamed x12 -> x6, local copies, waits for them, and re-layouts: 1.6 us -> 3.45 us
    convert_element_type x2 -> x1, other arithmetic: 1.34 us -> 0.07 us  [far_sum(): return (total.astype(BF16), arrived[0])]
    concatenate x6 -> x1, other arithmetic: 1.11 us -> 0.04 us  [far_gather(): block = jnp.concatenate(pairs, axis=1)]
    pallas_call x9 -> x5, Pallas kernels: 14.8 us -> 14.5 us  [the longest x2 8.01 us: weight_gradient(): pl.pallas_call(functools.partial(weight_kernel, first, scaled), out_shape...]
  transfers between devices with their start and end apart: 34 -> 18, of which waited for: 18 -> 10; matrix products, arithmetic and copies ran while one was open for 2% -> 1% of each run, Pallas kernels for 20% -> 14%
where the time goes in v1:
time: 102 us; the launch traced here: 101 us
  waiting for transfers between devices  50 us (49%)
  starting transfers between devices  22.3 us (22%)
  Pallas kernels  20.4 us (20%)
  local copies, waits for them, and re-layouts  4.4 us (4%)
  other arithmetic  3.22 us (3%)
    ppermute x18, waiting for transfers between devices, partner(): lax.ppermute(block, axis, [(i, i ^ mask) for i in range(lax.axis_size(axi...  50 us
    ppermute x18, starting transfers between devices, partner(): lax.ppermute(block, axis, [(i, i ^ mask) for i in range(lax.axis_size(axi...  22.3 us
    pallas_call x2, Pallas kernels, weight_gradient(): pl.pallas_call(functools.partial(weight_kernel, first, scaled), out_shape...  8.01 us
    pallas_call x1, Pallas kernels, on_device(): pl.pallas_call(hidden_kernel, out_shape=[jax.ShapeDtypeStruct((units, row...  4 us
    unnamed x6, local copies, waits for them, and re-layouts  3.45 us
    pallas_call x1, Pallas kernels, on_device(): pl.pallas_call(functools.partial(factor_kernel, experts), out_shape=[jax....  3.42 us
    pallas_call x1, Pallas kernels, on_device(): pl.pallas_call(output_kernel, out_shape=[jax.ShapeDtypeStruct((half_rows,...  3.04 us
  transfers between devices with their start and end apart: 18, of which 10 were waited for; matrix products, arithmetic and copies ran while one was open for 1% of the time, Pallas kernels for 14%

profile of v1, /device:TPU:0, one launch (start us, length us, event | category | flops | bytes accessed | tf_op | source)
XLA Modules:
  0.0 101.3 jit_solution(18436930036883292221)
XLA Ops:
  2.4 3.1 %collective-permute-start.2 = (bf16[16,4224]{1,0:T(8,128)(2,1)S(1)}, bf16[16,4224]{1,0:T(8,128)(2,1)S(1)}, u32[]{:S(2)}, u32[]{:S(2)}) collective-permute-start(bf16[16,4224]{1,0:T(8,128)(2,1)S(1)} %maximum_bitcast_fusion.2), channel_id=1, source_target_pairs={{0,4},{1,5},{2,6},{3,7},{4,0},{5,1},{6,2},{7,3},{8,12},{9,13},{10,... | collective-permute-start | bytes 405512 | tf_op jit(solution)/shard_map/ppermute | solution.py:251
  5.5 2.5 %collective-permute-start.1 = (bf16[16,4224]{1,0:T(8,128)(2,1)S(1)}, bf16[16,4224]{1,0:T(8,128)(2,1)S(1)}, u32[]{:S(2)}, u32[]{:S(2)}) collective-permute-start(bf16[16,4224]{1,0:T(8,128)(2,1)S(1)} %maximum_bitcast_fusion.2), channel_id=1, source_target_pairs={{0,12},{1,13},{2,14},{3,15},{4,8},{5,9},{6,10},{7,11},{8,4},{9,5},... | collective-permute-start | bytes 405512 | tf_op jit(solution)/shard_map/ppermute | solution.py:251
  9.1 6.3 %collective-permute-done.1 = bf16[16,4224]{1,0:T(8,128)(2,1)S(1)} collective-permute-done((bf16[16,4224]{1,0:T(8,128)(2,1)S(1)}, bf16[16,4224]{1,0:T(8,128)(2,1)S(1)}, u32[]{:S(2)}, u32[]{:S(2)}) %collective-permute-start.1) | collective-permute-done | bytes 135200 | tf_op jit(solution)/shard_map/ppermute | solution.py:251
  15.4 4.7 %collective-permute-done = bf16[16,4224]{1,0:T(8,128)(2,1)S(1)} collective-permute-done((bf16[16,4224]{1,0:T(8,128)(2,1)S(1)}, bf16[16,4224]{1,0:T(8,128)(2,1)S(1)}, u32[]{:S(2)}, u32[]{:S(2)}) %collective-permute-start) | collective-permute-done | bytes 135200 | tf_op jit(solution)/shard_map/ppermute | solution.py:251
  20.2 1.6 %collective-permute-start.3 = (bf16[32,4224]{1,0:T(8,128)(2,1)S(1)}, bf16[32,4224]{1,0:T(8,128)(2,1)S(1)}, u32[]{:S(2)}, u32[]{:S(2)}) collective-permute-start(bf16[32,4224]{1,0:T(8,128)(2,1)S(1)} %bitcast.75), channel_id=1, source_target_pairs={{0,2},{1,3},{2,0},{3,1},{4,6},{5,7},{6,4},{7,5},{8,10},{9,11},{10,... | collective-permute-start | bytes 811016 | tf_op jit(solution)/shard_map/ppermute | solution.py:251
  21.8 1.5 %collective-permute-start.6 = (bf16[32,4224]{1,0:T(8,128)(2,1)S(1)}, bf16[32,4224]{1,0:T(8,128)(2,1)S(1)}, u32[]{:S(2)}, u32[]{:S(2)}) collective-permute-start(bf16[32,4224]{1,0:T(8,128)(2,1)S(1)} %bitcast.81), channel_id=1, source_target_pairs={{0,16},{16,0},{1,17},{17,1},{2,18},{18,2},{3,19},{19,3},{4,20},{20... | collective-permute-start | bytes 811016 | tf_op jit(solution)/shard_map/ppermute | solution.py:251
  23.3 4.5 %collective-permute-done.3 = bf16[32,4224]{1,0:T(8,128)(2,1)S(1)} collective-permute-done((bf16[32,4224]{1,0:T(8,128)(2,1)S(1)}, bf16[32,4224]{1,0:T(8,128)(2,1)S(1)}, u32[]{:S(2)}, u32[]{:S(2)}) %collective-permute-start.3) | collective-permute-done | bytes 270368 | tf_op jit(solution)/shard_map/ppermute | solution.py:251
  27.9 1.6 %collective-permute-start.4 = (bf16[64,4224]{1,0:T(8,128)(2,1)S(1)}, bf16[64,4224]{1,0:T(8,128)(2,1)S(1)}, u32[]{:S(2)}, u32[]{:S(2)}) collective-permute-start(bf16[64,4224]{1,0:T(8,128)(2,1)S(1)} %maximum_bitcast_fusion.1), channel_id=1, source_target_pairs={{0,16},{16,0},{1,17},{17,1},{2,18},{18,2},{3,19},{19,3},{4,20},{20... | collective-permute-start | bytes 1622024 | tf_op jit(solution)/shard_map/ppermute | solution.py:251
  29.6 1.6 %collective-permute-start.7 = (bf16[64,4224]{1,0:T(8,128)(2,1)S(1)}, bf16[64,4224]{1,0:T(8,128)(2,1)S(1)}, u32[]{:S(2)}, u32[]{:S(2)}) collective-permute-start(bf16[64,4224]{1,0:T(8,128)(2,1)S(1)} %get-tuple-element.27), channel_id=1, source_target_pairs={{0,2},{1,3},{2,0},{3,1},{4,6},{5,7},{6,4},{7,5},{8,10},{9,11},{10,... | collective-permute-start | bytes 1622024 | tf_op jit(solution)/shard_map/ppermute | solution.py:251
  31.1 9.6 %collective-permute-done.4 = bf16[64,4224]{1,0:T(8,128)(2,1)S(1)} collective-permute-done((bf16[64,4224]{1,0:T(8,128)(2,1)S(1)}, bf16[64,4224]{1,0:T(8,128)(2,1)S(1)}, u32[]{:S(2)}, u32[]{:S(2)}) %collective-permute-start.4) | collective-permute-done | bytes 540704 | tf_op jit(solution)/shard_map/ppermute | solution.py:251
  43.0 2.8 %copy-done = bf16[1,2,384,4096]{3,2,1,0:T(8,128)(2,1)S(1)} copy-done((bf16[1,2,384,4096]{3,2,1,0:T(8,128)(2,1)S(1)}, bf16[1,2,384,4096]{3,2,1,0:T(8,128)(2,1)}, u32[]{:S(2)}) %copy-start) | copy-done | bytes 6291480
  45.8 1.6 %stage_in.1.win = bf16[768,4096]{1,0:T(8,128)(2,1)S(1)} custom-call(bf16[2,8,4224]{2,1,0:T(8,128)(2,1)S(1)} %bitcast.67, bf16[768,4096]{1,0:T(8,128)(2,1)S(1)} %bitcast.63), custom_call_target="tpu_custom_call" | custom-call | bytes 12582912 | tf_op jit(solution)/shard_map/stage_in/pallas_call | solution.py:332
  47.4 4.0 %hidden.1 = (bf16[384,256]{1,0:T(8,128)(2,1)S(1)}, f32[384,256]{1,0:T(8,128)S(1)}, f32[384,256]{1,0:T(8,128)S(1)}) custom-call(bf16[128,4224]{1,0:T(8,128)(2,1)S(1)} %maximum_bitcast_fusion.xa.ra, bf16[128,4224]{1,0:T(8,128)(2,1)S(1)} %collective-permute-done.5.xb.rb, bf16[768,4096]{1,0:T(8,128)(2,1)S(1)} %stage_in.1.win, ...), custom_call_target="tpu_custom_call" | custom-call | flops 1610612736 | bytes 10485760 | tf_op jit(solution)/shard_map/hidden/pallas_call | solution.py:356
  51.4 3.4 %factors.1 = (bf16[1152,256]{1,0:T(8,128)(2,1)S(1)}, f32[256,128]{1,0:T(8,128)S(1)}, f32[256,128]{1,0:T(8,128)S(1)}) custom-call(s32[16]{0:T(128)S(1)} %copy-done.2, bf16[128,4224]{1,0:T(8,128)(2,1)S(1)} %maximum_bitcast_fusion.xa.ra, bf16[128,4224]{1,0:T(8,128)(2,1)S(1)} %collective-permute-done.5.xb.rb, bf16[128,4224]{1,0:T(8,128)(2,1)S(1)} %bitcast.61, ...), custom_call_target="tpu_custom_call" | custom-call | flops 805306368 | bytes 5242880 | tf_op jit(solution)/shard_map/factors/pallas_call | solution.py:374
  54.8 3.0 %outputs.1 = (bf16[128,4096]{1,0:T(8,128)(2,1)S(1)}, bf16[128,4096]{1,0:T(8,128)(2,1)S(1)}, bf16[128,8192]{1,0:T(8,128)(2,1)S(1)}) custom-call(f32[256,128]{1,0:T(8,128)S(1)} %get-tuple-element.16.gate, bf16[1152,256]{1,0:T(8,128)(2,1)S(1)} %get-tuple-element.17.factors.own, bf16[768,4096]{1,0:T(8,128)(2,1)S(1)} %stage_in.1.win, ...), custom_call_target="tpu_custom_call" | custom-call | flops 2415919104 | bytes 15728640 | tf_op jit(solution)/shard_map/outputs/pallas_call | solution.py:390
  58.0 4.1 %collective-permute-done.9 = bf16[128,8192]{1,0:T(8,128)(2,1)S(1)} collective-permute-done((bf16[128,8192]{1,0:T(8,128)(2,1)S(1)}, bf16[128,8192]{1,0:T(8,128)(2,1)S(1)}, u32[]{:S(2)}, u32[]{:S(2)}) %collective-permute-start.9) | collective-permute-done | bytes 2097184 | tf_op jit(solution)/shard_map/ppermute | solution.py:251
  64.0 1.6 %collective-permute-start.10 = (bf16[64,4096]{1,0:T(8,128)(2,1)S(1)}, bf16[64,4096]{1,0:T(8,128)(2,1)S(1)}, u32[]{:S(2)}, u32[]{:S(2)}) collective-permute-start(bf16[64,4096]{1,0:T(8,128)(2,1)S(1)} %get-tuple-element.23), channel_id=1, source_target_pairs={{0,16},{16,0},{1,17},{17,1},{2,18},{18,2},{3,19},{19,3},{4,20},{20... | collective-permute-start | bytes 1572872 | tf_op jit(solution)/shard_map/ppermute | solution.py:251
  65.7 10.8 %collective-permute-done.13 = bf16[64,4096]{1,0:T(8,128)(2,1)S(1)} collective-permute-done((bf16[64,4096]{1,0:T(8,128)(2,1)S(1)}, bf16[64,4096]{1,0:T(8,128)(2,1)S(1)}, u32[]{:S(2)}, u32[]{:S(2)}) %collective-permute-start.13) | collective-permute-done | bytes 524320 | tf_op jit(solution)/shard_map/ppermute | solution.py:251
  76.6 1.6 %collective-permute-start.14 = (bf16[32,4096]{1,0:T(8,128)(2,1)S(1)}, bf16[32,4096]{1,0:T(8,128)(2,1)S(1)}, u32[]{:S(2)}, u32[]{:S(2)}) collective-permute-start(bf16[32,4096]{1,0:T(8,128)(2,1)S(1)} %fusion.7.refs_2_), channel_id=1, source_target_pairs={{0,16},{16,0},{1,17},{17,1},{2,18},{18,2},{3,19},{19,3},{4,20},{20... | collective-permute-start | bytes 786440 | tf_op jit(solution)/shard_map/ppermute | solution.py:251
  79.5 7.5 %collective-permute-done.12.refs_0_.away = bf16[1152,256]{1,0:T(8,128)(2,1)S(1)} collective-permute-done((bf16[1152,256]{1,0:T(8,128)(2,1)S(1)}, bf16[1152,256]{1,0:T(8,128)(2,1)S(1)}, u32[]{:S(2)}, u32[]{:S(2)}) %collective-permute-start.12) | collective-permute-done | bytes 589856 | tf_op jit(solution)/shard_map/ppermute | solution.py:251
  87.6 1.9 %collective-permute-start.16 = (bf16[8,8192]{1,0:T(8,128)(2,1)S(1)}, bf16[8,8192]{1,0:T(8,128)(2,1)S(1)}, u32[]{:S(2)}, u32[]{:S(2)}) collective-permute-start(bf16[8,8192]{1,0:T(8,128)(2,1)S(1)} %get-tuple-element.34.rest_1_), channel_id=1, source_target_pairs={{0,8},{1,9},{2,10},{3,11},{4,12},{5,13},{6,14},{7,15},{8,0},{9,1},... | collective-permute-start | bytes 393224 | tf_op jit(solution)/shard_map/ppermute | solution.py:251
  89.5 2.4 %collective-permute-start.17 = (bf16[8,8192]{1,0:T(8,128)(2,1)S(1)}, bf16[8,8192]{1,0:T(8,128)(2,1)S(1)}, u32[]{:S(2)}, u32[]{:S(2)}) collective-permute-start(bf16[8,8192]{1,0:T(8,128)(2,1)S(1)} %get-tuple-element.35.rest_2_), channel_id=1, source_target_pairs={{0,12},{1,13},{2,14},{3,15},{4,8},{5,9},{6,10},{7,11},{8,4},{9,5},... | collective-permute-start | bytes 393224 | tf_op jit(solution)/shard_map/ppermute | solution.py:251
  91.9 3.7 %grad_down.1 = bf16[1,384,4096]{2,1,0:T(8,128)(2,1)} custom-call(s32[16]{0:T(128)S(1)} %copy-done.2, bf16[1152,256]{1,0:T(8,128)(2,1)S(1)} %get-tuple-element.17.factors.own, bf16[1152,256]{1,0:T(8,128)(2,1)S(1)} %collective-permute-done.12.refs_0_.away, f32[256,128]{1,0:T(8,128)S(1)} %get-tuple-element.21.gate, bf16[128,4224]{1,0:T(8,128)(2,1)S(1)} %bitcast.62, ...), custom_call_target="tpu_custom_call" | custom-call | flops 805306368 | bytes 5242880 | tf_op jit(solution)/shard_map/grad_down/pallas_call | solution.py:455
  95.6 4.3 %grad_in.1 = bf16[2,384,4096]{2,1,0:T(8,128)(2,1)} custom-call(s32[16]{0:T(128)S(1)} %copy-done.2, bf16[1152,256]{1,0:T(8,128)(2,1)S(1)} %get-tuple-element.17.factors.own, bf16[1152,256]{1,0:T(8,128)(2,1)S(1)} %collective-permute-done.12.refs_0_.away, f32[256,128]{1,0:T(8,128)S(1)} %get-tuple-element.21.gate, ...), custom_call_target="tpu_custom_call" | custom-call | flops 1610612736 | bytes 8388608 | tf_op jit(solution)/shard_map/grad_in/pallas_call | solution.py:455
  (50 shorter events, 10.8 us)
Async XLA Ops:
  2.4 6.7 %collective-permute-start.2 = (bf16[16,4224]{1,0:T(8,128)(2,1)S(1)}, bf16[16,4224]{1,0:T(8,128)(2,1)S(1)}, u32[]{:S(2)}, u32[]{:S(2)}) collective-permute-start(bf16[16,4224]{1,0:T(8,128)(2,1)S(1)} %maximum_bitcast_fusion.2), channel_id=1, source_target_pairs={{0,4},{1,5},{2,6},{3,7},{4,0},{5,1},{6,2},{7,3},{8,12},{9,13},{10,... | collective-permute-start | bytes 405512 | tf_op jit(solution)/shard_map/ppermute | solution.py:251
  5.5 9.9 %collective-permute-start.1 = (bf16[16,4224]{1,0:T(8,128)(2,1)S(1)}, bf16[16,4224]{1,0:T(8,128)(2,1)S(1)}, u32[]{:S(2)}, u32[]{:S(2)}) collective-permute-start(bf16[16,4224]{1,0:T(8,128)(2,1)S(1)} %maximum_bitcast_fusion.2), channel_id=1, source_target_pairs={{0,12},{1,13},{2,14},{3,15},{4,8},{5,9},{6,10},{7,11},{8,4},{9,5},... | collective-permute-start | bytes 405512 | tf_op jit(solution)/shard_map/ppermute | solution.py:251
  8.0 12.1 %collective-permute-start = (bf16[16,4224]{1,0:T(8,128)(2,1)S(1)}, bf16[16,4224]{1,0:T(8,128)(2,1)S(1)}, u32[]{:S(2)}, u32[]{:S(2)}) collective-permute-start(bf16[16,4224]{1,0:T(8,128)(2,1)S(1)} %maximum_bitcast_fusion.2), channel_id=1, source_target_pairs={{0,8},{1,9},{2,10},{3,11},{4,12},{5,13},{6,14},{7,15},{8,0},{9,1},... | collective-permute-start | bytes 405512 | tf_op jit(solution)/shard_map/ppermute | solution.py:251
  20.2 7.6 %collective-permute-start.3 = (bf16[32,4224]{1,0:T(8,128)(2,1)S(1)}, bf16[32,4224]{1,0:T(8,128)(2,1)S(1)}, u32[]{:S(2)}, u32[]{:S(2)}) collective-permute-start(bf16[32,4224]{1,0:T(8,128)(2,1)S(1)} %bitcast.75), channel_id=1, source_target_pairs={{0,2},{1,3},{2,0},{3,1},{4,6},{5,7},{6,4},{7,5},{8,10},{9,11},{10,... | collective-permute-start | bytes 811016 | tf_op jit(solution)/shard_map/ppermute | solution.py:251
  21.8 7.6 %collective-permute-start.6 = (bf16[32,4224]{1,0:T(8,128)(2,1)S(1)}, bf16[32,4224]{1,0:T(8,128)(2,1)S(1)}, u32[]{:S(2)}, u32[]{:S(2)}) collective-permute-start(bf16[32,4224]{1,0:T(8,128)(2,1)S(1)} %bitcast.81), channel_id=1, source_target_pairs={{0,16},{16,0},{1,17},{17,1},{2,18},{18,2},{3,19},{19,3},{4,20},{20... | collective-permute-start | bytes 811016 | tf_op jit(solution)/shard_map/ppermute | solution.py:251
  27.9 12.8 %collective-permute-start.4 = (bf16[64,4224]{1,0:T(8,128)(2,1)S(1)}, bf16[64,4224]{1,0:T(8,128)(2,1)S(1)}, u32[]{:S(2)}, u32[]{:S(2)}) collective-permute-start(bf16[64,4224]{1,0:T(8,128)(2,1)S(1)} %maximum_bitcast_fusion.1), channel_id=1, source_target_pairs={{0,16},{16,0},{1,17},{17,1},{2,18},{18,2},{3,19},{19,3},{4,20},{20... | collective-permute-start | bytes 1622024 | tf_op jit(solution)/shard_map/ppermute | solution.py:251
  29.6 12.2 %collective-permute-start.7 = (bf16[64,4224]{1,0:T(8,128)(2,1)S(1)}, bf16[64,4224]{1,0:T(8,128)(2,1)S(1)}, u32[]{:S(2)}, u32[]{:S(2)}) collective-permute-start(bf16[64,4224]{1,0:T(8,128)(2,1)S(1)} %get-tuple-element.27), channel_id=1, source_target_pairs={{0,2},{1,3},{2,0},{3,1},{4,6},{5,7},{6,4},{7,5},{8,10},{9,11},{10,... | collective-permute-start | bytes 1622024 | tf_op jit(solution)/shard_map/ppermute | solution.py:251
  40.7 1.9 %copy-start.1 = (bf16[1,384,4096]{2,1,0:T(8,128)(2,1)S(1)}, bf16[1,384,4096]{2,1,0:T(8,128)(2,1)}, u32[]{:S(2)}) copy-start(bf16[1,384,4096]{2,1,0:T(8,128)(2,1)} %param.13) | copy-start | bytes 9437188
  40.8 6.6 %collective-permute-start.5 = (bf16[128,4224]{1,0:T(8,128)(2,1)S(1)}, bf16[128,4224]{1,0:T(8,128)(2,1)S(1)}, u32[]{:S(2)}, u32[]{:S(2)}) collective-permute-start(bf16[128,4224]{1,0:T(8,128)(2,1)S(1)} %maximum_bitcast_fusion.xa.ra), channel_id=1, source_target_pairs={{0,1},{1,0},{2,3},{3,2},{4,5},{5,4},{6,7},{7,6},{8,9},{9,8},{10,11... | collective-permute-start | bytes 3244040 | tf_op jit(solution)/shard_map/ppermute | solution.py:251
  41.8 9.6 %collective-permute-start.8 = (bf16[128,4224]{1,0:T(8,128)(2,1)S(1)}, bf16[128,4224]{1,0:T(8,128)(2,1)S(1)}, u32[]{:S(2)}, u32[]{:S(2)}) collective-permute-start(bf16[128,4224]{1,0:T(8,128)(2,1)S(1)} %bitcast.60), channel_id=1, source_target_pairs={{0,1},{1,0},{2,3},{3,2},{4,5},{5,4},{6,7},{7,6},{8,9},{9,8},{10,11... | collective-permute-start | bytes 3244040 | tf_op jit(solution)/shard_map/ppermute | solution.py:251
  43.0 2.8 %copy-start = (bf16[1,2,384,4096]{3,2,1,0:T(8,128)(2,1)S(1)}, bf16[1,2,384,4096]{3,2,1,0:T(8,128)(2,1)}, u32[]{:S(2)}) copy-start(bf16[1,2,384,4096]{3,2,1,0:T(8,128)(2,1)} %param.12) | copy-start | bytes 18874372
  47.4 4.0 %copy-start.2 = (s32[16]{0:T(128)S(1)}, s32[16]{0:T(128)}, u32[]{:S(2)}) copy-start(s32[16]{0:T(128)} %flags.5) | copy-start | bytes 196
  57.9 4.2 %collective-permute-start.9 = (bf16[128,8192]{1,0:T(8,128)(2,1)S(1)}, bf16[128,8192]{1,0:T(8,128)(2,1)S(1)}, u32[]{:S(2)}, u32[]{:S(2)}) collective-permute-start(bf16[128,8192]{1,0:T(8,128)(2,1)S(1)} %get-tuple-element.19), channel_id=1, source_target_pairs={{0,1},{1,0},{2,3},{3,2},{4,5},{5,4},{6,7},{7,6},{8,9},{9,8},{10,11... | collective-permute-start | bytes 6291464 | tf_op jit(solution)/shard_map/ppermute | solution.py:251
  58.0 29.1 %collective-permute-start.12 = (bf16[1152,256]{1,0:T(8,128)(2,1)S(1)}, bf16[1152,256]{1,0:T(8,128)(2,1)S(1)}, u32[]{:S(2)}, u32[]{:S(2)}) collective-permute-start(bf16[1152,256]{1,0:T(8,128)(2,1)S(1)} %get-tuple-element.17.factors.own), channel_id=1, source_target_pairs={{0,8},{1,9},{2,10},{3,11},{4,12},{5,13},{6,14},{7,15},{8,0},{9,1},... | collective-permute-start | bytes 1769480 | tf_op jit(solution)/shard_map/ppermute | solution.py:251
  62.5 14.0 %collective-permute-start.13 = (bf16[64,4096]{1,0:T(8,128)(2,1)S(1)}, bf16[64,4096]{1,0:T(8,128)(2,1)S(1)}, u32[]{:S(2)}, u32[]{:S(2)}) collective-permute-start(bf16[64,4096]{1,0:T(8,128)(2,1)S(1)} %bitcast.84), channel_id=1, source_target_pairs={{0,2},{1,3},{2,0},{3,1},{4,6},{5,7},{6,4},{7,5},{8,10},{9,11},{10,... | collective-permute-start | bytes 1572872 | tf_op jit(solution)/shard_map/ppermute | solution.py:251
  64.0 14.1 %collective-permute-start.10 = (bf16[64,4096]{1,0:T(8,128)(2,1)S(1)}, bf16[64,4096]{1,0:T(8,128)(2,1)S(1)}, u32[]{:S(2)}, u32[]{:S(2)}) collective-permute-start(bf16[64,4096]{1,0:T(8,128)(2,1)S(1)} %get-tuple-element.23), channel_id=1, source_target_pairs={{0,16},{16,0},{1,17},{17,1},{2,18},{18,2},{3,19},{19,3},{4,20},{20... | collective-permute-start | bytes 1572872 | tf_op jit(solution)/shard_map/ppermute | solution.py:251
  76.6 10.5 %collective-permute-start.14 = (bf16[32,4096]{1,0:T(8,128)(2,1)S(1)}, bf16[32,4096]{1,0:T(8,128)(2,1)S(1)}, u32[]{:S(2)}, u32[]{:S(2)}) collective-permute-start(bf16[32,4096]{1,0:T(8,128)(2,1)S(1)} %fusion.7.refs_2_), channel_id=1, source_target_pairs={{0,16},{16,0},{1,17},{17,1},{2,18},{18,2},{3,19},{19,3},{4,20},{20... | collective-permute-start | bytes 786440 | tf_op jit(solution)/shard_map/ppermute | solution.py:251
  78.2 8.9 %collective-permute-start.11 = (bf16[32,4096]{1,0:T(8,128)(2,1)S(1)}, bf16[32,4096]{1,0:T(8,128)(2,1)S(1)}, u32[]{:S(2)}, u32[]{:S(2)}) collective-permute-start(bf16[32,4096]{1,0:T(8,128)(2,1)S(1)} %fusion.6.refs_1_), channel_id=1, source_target_pairs={{0,2},{1,3},{2,0},{3,1},{4,6},{5,7},{6,4},{7,5},{8,10},{9,11},{10,... | collective-permute-start | bytes 786440 | tf_op jit(solution)/shard_map/ppermute | solution.py:251
  87.5 12.5 %collective-permute-start.15 = (bf16[8,8192]{1,0:T(8,128)(2,1)S(1)}, bf16[8,8192]{1,0:T(8,128)(2,1)S(1)}, u32[]{:S(2)}, u32[]{:S(2)}) collective-permute-start(bf16[8,8192]{1,0:T(8,128)(2,1)S(1)} %slice.130.rest_0_), channel_id=1, source_target_pairs={{0,4},{1,5},{2,6},{3,7},{4,0},{5,1},{6,2},{7,3},{8,12},{9,13},{10,... | collective-permute-start | bytes 393224 | tf_op jit(solution)/shard_map/ppermute | solution.py:251
  87.6 13.0 %collective-permute-start.16 = (bf16[8,8192]{1,0:T(8,128)(2,1)S(1)}, bf16[8,8192]{1,0:T(8,128)(2,1)S(1)}, u32[]{:S(2)}, u32[]{:S(2)}) collective-permute-start(bf16[8,8192]{1,0:T(8,128)(2,1)S(1)} %get-tuple-element.34.rest_1_), channel_id=1, source_target_pairs={{0,8},{1,9},{2,10},{3,11},{4,12},{5,13},{6,14},{7,15},{8,0},{9,1},... | collective-permute-start | bytes 393224 | tf_op jit(solution)/shard_map/ppermute | solution.py:251
  89.5 11.0 %collective-permute-start.17 = (bf16[8,8192]{1,0:T(8,128)(2,1)S(1)}, bf16[8,8192]{1,0:T(8,128)(2,1)S(1)}, u32[]{:S(2)}, u32[]{:S(2)}) collective-permute-start(bf16[8,8192]{1,0:T(8,128)(2,1)S(1)} %get-tuple-element.35.rest_2_), channel_id=1, source_target_pairs={{0,12},{1,13},{2,14},{3,15},{4,8},{5,9},{6,10},{7,11},{8,4},{9,5},... | collective-permute-start | bytes 393224 | tf_op jit(solution)/shard_map/ppermute | solution.py:251
